TPU v7x, 32 devices: a whole 2x2x4 slice. The times are simulated.
32 devices in a mesh: member: 2 (over y), gx: 4 (over z), gy: 4 (over x, core).
Axes of the slice: x: 2, y: 2, z: 4, core: 2. Of those that a mesh axis runs over, the one named last changes fastest.
Arguments:
- checkpoint: float32 [8, 4, 4, 12288], P(('member', 'gx'), 'gy'), parts along dimension 0, may hold values from -6 to 6
- holder_list: int32 [8, 4, 4], P(('member', 'gx'), 'gy'), parts along dimension 0, may hold values from 0 to 3, each once within a row
- height: float32 [64, 512], P(('member', 'gx'), 'gy'), parts along dimension 0, may hold values from -6 to 6
- land_mask: int32 [32, 512], P('gx', 'gy'), may hold values 0 or 1
- diffusivity: float32 [3, 16], replicated, may hold values from 0.02 to 0.2
- tracer_weight: float32 [6, 16, 32, 512], P('member', None, 'gx', 'gy'), parts along dimension 0, may hold values from -6 to 6
- height_weight: float32 [64, 512], P(('member', 'gx'), 'gy'), parts along dimension 0, may hold values from -6 to 6
Outputs:
- adjoint_tracers: float32 [6, 16, 32, 512], P('member', None, 'gx', 'gy'), parts along dimension 0
- adjoint_height: float32 [64, 512], P(('member', 'gx'), 'gy'), parts along dimension 0
There are 2 independent parts, one for each index of `member`. A program takes and returns all parts, laid end to end along the dimension named above; an argument that names none is the same for every part. Nothing has to cross between parts.
Inputs may be any that keep to these rules, and one draw needn't show every extreme that they name: For each owner device (o, g), holder_list[o, g, :] names every longitude index once: each device along gx holds exactly one piece of every owner's tracers in its row.
All inputs are finite; a program needn't handle non-finite values. No bound on the sum of `land_mask` on one device may be relied on, other than what follows from the above.
Results may differ from a plain program's by a relative error of at most 0.0001.
Values sent between devices are 32-bit elements; how exact they have to be, the bound alone decides.
A program may use at most 64 MiB of HBM per device.

v0:
```python
import jax
import jax.numpy as jnp
from jax import lax
from jax.sharding import PartitionSpec as P

ITERS = 4


ADVECTION = 0.3
VERTICAL_MIX = 0.1
HEIGHT_DIFFUSION = 0.2
HEIGHT_DAMPING = 0.3
BUOYANCY = 0.5


def padded_2(cells, sides, width):
    for axis, dim in sides:
        count = lax.axis_size(axis)
        head = lax.slice_in_dim(cells, 0, width, axis=dim)
        tail = lax.slice_in_dim(cells, cells.shape[dim] - width, cells.shape[dim], axis=dim)
        cells = jnp.concatenate(
            [
                lax.ppermute(tail, axis, [(i, (i + 1) % count) for i in range(count)]),
                cells,
                lax.ppermute(head, axis, [((i + 1) % count, i) for i in range(count)]),
            ],
            axis=dim,
        )
    return cells


def shifted(block, axis, distance):
    devices = range(lax.axis_size(axis))
    route = [((i - distance) % len(devices), i) for i in devices]
    return lax.ppermute(block, axis, route)


def shifted_2(value, axis, steps):
    count = lax.axis_size(axis)
    initial, last = (max(0, -steps), min(count, count - steps))
    return lax.ppermute(value, axis, [(source, source + steps) for source in range(initial, last)])


def advance(height_pad, tracer_pad, wet_cells, diffusivity):
    east_cell = tracer_pad[..., 2:, 1:-1]
    west_cell = tracer_pad[..., :-2, 1:-1]
    north_cell = tracer_pad[..., 1:-1, 2:]
    south_cell = tracer_pad[..., 1:-1, :-2]
    centre = tracer_pad[..., 1:-1, 1:-1]
    height_mid = height_pad[1:-1, 1:-1]
    zonal = -0.5 * (height_pad[1:-1, 2:] - height_pad[1:-1, :-2])
    meridional = 0.5 * (height_pad[2:, 1:-1] - height_pad[:-2, 1:-1])
    advect = zonal * 0.5 * (east_cell - west_cell) + meridional * 0.5 * (north_cell - south_cell)
    laplace = east_cell + west_cell + north_cell + south_cell - 4.0 * centre
    upper = jnp.concatenate([centre[:, :1], centre[:, :-1]], axis=1)
    lower = jnp.concatenate([centre[:, 1:], centre[:, -1:]], axis=1)
    vertical = upper + lower - 2.0 * centre
    tracer_new = centre + wet_cells * (
        -ADVECTION * advect + diffusivity[:, :, None, None] * laplace + VERTICAL_MIX * vertical
    )
    height_lap = (
        height_pad[2:, 1:-1]
        + height_pad[:-2, 1:-1]
        + height_pad[1:-1, 2:]
        + height_pad[1:-1, :-2]
        - 4.0 * height_mid
    )
    height_new = (
        height_mid
        + HEIGHT_DIFFUSION * height_lap
        - HEIGHT_DAMPING * jnp.tanh(height_mid)
        + BUOYANCY * wet_cells * jnp.mean(centre[0], axis=0)
    )
    return (height_new, tracer_new)


def local(checkpoint, holder_list, height, land_mask, diffusivity, tracer_weight, height_weight):
    width_x, width_y = height.shape
    levels = diffusivity.shape[1]
    channels = 3 * levels
    received = lax.all_to_all(checkpoint, "gx", split_axis=2, concat_axis=0, tiled=True)
    pieces = received.reshape(received.shape[0], received.shape[3])
    tracers = jnp.take(pieces, holder_list[0, 0], axis=0).reshape(3, levels, width_x, width_y)
    wet_cells = land_mask.astype(jnp.float32)
    lat_index = lax.axis_index("gy")
    lat_count = lax.axis_size("gy")
    saved = []
    column = jnp.arange(width_y + 2)
    keep_cols = (
        ((column > 0) | (lat_index > 0)) & ((column < width_y + 1) | (lat_index < lat_count - 1))
    ).astype(jnp.float32)
    height_now, tracer_now = (height, tracers)
    for repeat in range(ITERS):
        stacked = jnp.concatenate(
            [tracer_now.reshape(channels, width_x, width_y), height_now[None]], axis=0
        )
        padded = padded_2(stacked, (("gx", 1), ("gy", 2)), 1) * keep_cols
        height_pad = padded[channels]
        tracer_pad = padded[:channels].reshape(3, levels, width_x + 2, width_y + 2)
        saved.append((height_pad, tracer_pad))
        height_now, tracer_now = advance(height_pad, tracer_pad, wet_cells, diffusivity)
    adjoint_height, adjoint_tracers = (height_weight, tracer_weight)
    for repeat in reversed(range(ITERS)):
        height_pad, tracer_pad = saved[repeat]

        def local_step(height_field, tracer_field):
            return advance(height_field, tracer_field, wet_cells, diffusivity)

        outputs, pullback = jax.vjp(local_step, height_pad, tracer_pad)
        grad_height, grad_tracer = pullback((adjoint_height, adjoint_tracers))
        gradients = jnp.concatenate(
            [grad_tracer.reshape(channels, width_x + 2, width_y + 2), grad_height[None]], axis=0
        )
        interior = gradients[:, 1:-1, 1:-1]
        west_rim = gradients[:, 0, 1:-1]
        east_rim = gradients[:, -1, 1:-1]
        south_rim = gradients[:, 1:-1, 0]
        north_rim = gradients[:, 1:-1, -1]
        from_east = shifted(west_rim, "gx", -1)
        from_west = shifted(east_rim, "gx", 1)
        from_north = shifted_2(south_rim, "gy", -1)
        from_south = shifted_2(north_rim, "gy", 1)
        summed = interior.at[:, -1, :].add(from_east).at[:, 0, :].add(from_west)
        summed = summed.at[:, :, -1].add(from_north).at[:, :, 0].add(from_south)
        adjoint_tracers = summed[:channels].reshape(3, levels, width_x, width_y)
        adjoint_height = summed[channels]
    return (adjoint_tracers, adjoint_height)


def solution(mesh):
    return jax.shard_map(
        local,
        mesh=mesh,
        in_specs=(
            P(("member", "gx"), "gy", None, None),
            P(("member", "gx"), "gy", None),
            P(("member", "gx"), "gy"),
            P("gx", "gy"),
            P(),
            P("member", None, "gx", "gy"),
            P(("member", "gx"), "gy"),
        ),
        out_specs=(P("member", None, "gx", "gy"), P(("member", "gx"), "gy")),
        check_vma=False,
    )
```

profile of v0, /device:TPU:0, one launch (start us, length us, event | category | flops | bytes accessed | tf_op | source)
XLA Modules:
  0.0 166.1 jit_solution(3557801926332634943)
XLA Ops:
  0.6 1.8 %copy.263 = f32[1,1,4,12288]{3,1,0,2:T(1,128)} copy(f32[1,1,4,12288]{3,2,1,0:T(4,128)} %param.39) | data formatting | bytes 393216 | tf_op args[0]
  2.4 6.4 %all-to-all-start = ((f32[1,1,4,12288]{3,1,0,2:T(1,128)}), f32[1,1,4,12288]{3,1,0,2:T(1,128)S(1)}, u32[]{:S(2)}, u32[]{:S(2)}) async-start(f32[1,1,4,12288]{3,1,0,2:T(1,128)} %copy.263), calls=%async_computation | async-start | bytes 393216 | tf_op jit(solution)/shard_map/all_to_all | solution.py:81
  9.1 7.3 %all-to-all-done = f32[1,1,4,12288]{3,1,0,2:T(1,128)S(1)} async-done(((f32[1,1,4,12288]{3,1,0,2:T(1,128)}), f32[1,1,4,12288]{3,1,0,2:T(1,128)S(1)}, u32[]{:S(2)}, u32[]{:S(2)}) %all-to-all-start) | async-done | bytes 196640 | tf_op jit(solution)/shard_map/all_to_all | solution.py:81
  20.1 1.8 %collective-permute-done.1 = f32[49,1,128]{2,1,0:T(1,128)S(1)} collective-permute-done((f32[49,1,128]{2,1,0:T(1,128)S(1)}, f32[49,1,128]{2,1,0:T(1,128)S(1)}, u32[]{:S(2)}, u32[]{:S(2)}) %collective-permute-start.1) | collective-permute-done | bytes 25120 | tf_op jit(solution)/shard_map/ppermute | solution.py:25
  21.9 3.2 %collective-permute-done = f32[49,1,128]{2,1,0:T(1,128)S(1)} collective-permute-done((f32[49,1,128]{2,1,0:T(1,128)S(1)}, f32[49,1,128]{2,1,0:T(1,128)S(1)}, u32[]{:S(2)}, u32[]{:S(2)}) %collective-permute-start) | collective-permute-done | bytes 25120 | tf_op jit(solution)/shard_map/ppermute | solution.py:23
  26.1 8.1 %collective-permute-done.3 = f32[49,10,1]{2,1,0:T(8,128)S(1)} collective-permute-done((f32[49,10,1]{2,1,0:T(8,128)S(1)}, f32[49,10,1]{2,1,0:T(8,128)S(1)}, u32[]{:S(2)}, u32[]{:S(2)}) %collective-permute-start.3) | collective-permute-done | bytes 1992 | tf_op jit(solution)/shard_map/ppermute | solution.py:25
  34.2 2.9 %collective-permute-done.2 = f32[49,10,1]{2,1,0:T(8,128)S(1)} collective-permute-done((f32[49,10,1]{2,1,0:T(8,128)S(1)}, f32[49,10,1]{2,1,0:T(8,128)S(1)}, u32[]{:S(2)}, u32[]{:S(2)}) %collective-permute-start.2) | collective-permute-done | bytes 1992 | tf_op jit(solution)/shard_map/ppermute | solution.py:23
  40.0 2.0 %collective-permute-start.4 = (f32[49,1,128]{2,1,0:T(1,128)S(1)}, f32[49,1,128]{2,1,0:T(1,128)S(1)}, u32[]{:S(2)}, u32[]{:S(2)}) collective-permute-start(f32[49,1,128]{2,1,0:T(1,128)S(1)} %get-tuple-element.302), channel_id=1, source_target_pairs={{0,4},{4,8},{8,12},{12,0},{1,5},{5,9},{9,13},{13,1},{2,6},{6,10},{... | collective-permute-start | bytes 75272 | tf_op jit(solution)/shard_map/ppermute | solution.py:23
  42.0 1.8 %collective-permute-done.5 = f32[49,1,128]{2,1,0:T(1,128)S(1)} collective-permute-done((f32[49,1,128]{2,1,0:T(1,128)S(1)}, f32[49,1,128]{2,1,0:T(1,128)S(1)}, u32[]{:S(2)}, u32[]{:S(2)}) %collective-permute-start.5) | collective-permute-done | bytes 25120 | tf_op jit(solution)/shard_map/ppermute | solution.py:25
  43.8 1.9 %collective-permute-done.4 = f32[49,1,128]{2,1,0:T(1,128)S(1)} collective-permute-done((f32[49,1,128]{2,1,0:T(1,128)S(1)}, f32[49,1,128]{2,1,0:T(1,128)S(1)}, u32[]{:S(2)}, u32[]{:S(2)}) %collective-permute-start.4) | collective-permute-done | bytes 25120 | tf_op jit(solution)/shard_map/ppermute | solution.py:23
  46.5 9.2 %collective-permute-done.7 = f32[49,10,1]{2,1,0:T(8,128)S(1)} collective-permute-done((f32[49,10,1]{2,1,0:T(8,128)S(1)}, f32[49,10,1]{2,1,0:T(8,128)S(1)}, u32[]{:S(2)}, u32[]{:S(2)}) %collective-permute-start.7) | collective-permute-done | bytes 1992 | tf_op jit(solution)/shard_map/ppermute | solution.py:25
  59.1 1.8 %collective-permute-start.8 = (f32[49,1,128]{2,1,0:T(1,128)S(1)}, f32[49,1,128]{2,1,0:T(1,128)S(1)}, u32[]{:S(2)}, u32[]{:S(2)}) collective-permute-start(f32[49,1,128]{2,1,0:T(1,128)S(1)} %get-tuple-element.300), channel_id=1, source_target_pairs={{0,4},{4,8},{8,12},{12,0},{1,5},{5,9},{9,13},{13,1},{2,6},{6,10},{... | collective-permute-start | bytes 75272 | tf_op jit(solution)/shard_map/ppermute | solution.py:23
  60.9 1.8 %collective-permute-done.9 = f32[49,1,128]{2,1,0:T(1,128)S(1)} collective-permute-done((f32[49,1,128]{2,1,0:T(1,128)S(1)}, f32[49,1,128]{2,1,0:T(1,128)S(1)}, u32[]{:S(2)}, u32[]{:S(2)}) %collective-permute-start.9) | collective-permute-done | bytes 25120 | tf_op jit(solution)/shard_map/ppermute | solution.py:25
  62.7 2.0 %collective-permute-done.8 = f32[49,1,128]{2,1,0:T(1,128)S(1)} collective-permute-done((f32[49,1,128]{2,1,0:T(1,128)S(1)}, f32[49,1,128]{2,1,0:T(1,128)S(1)}, u32[]{:S(2)}, u32[]{:S(2)}) %collective-permute-start.8) | collective-permute-done | bytes 25120 | tf_op jit(solution)/shard_map/ppermute | solution.py:23
  65.6 8.4 %collective-permute-done.11 = f32[49,10,1]{2,1,0:T(8,128)S(1)} collective-permute-done((f32[49,10,1]{2,1,0:T(8,128)S(1)}, f32[49,10,1]{2,1,0:T(8,128)S(1)}, u32[]{:S(2)}, u32[]{:S(2)}) %collective-permute-start.11) | collective-permute-done | bytes 1992 | tf_op jit(solution)/shard_map/ppermute | solution.py:25
  74.0 2.5 %collective-permute-done.10 = f32[49,10,1]{2,1,0:T(8,128)S(1)} collective-permute-done((f32[49,10,1]{2,1,0:T(8,128)S(1)}, f32[49,10,1]{2,1,0:T(8,128)S(1)}, u32[]{:S(2)}, u32[]{:S(2)}) %collective-permute-start.10) | collective-permute-done | bytes 1992 | tf_op jit(solution)/shard_map/ppermute | solution.py:23
  78.0 2.0 %collective-permute-start.12 = (f32[49,1,128]{2,1,0:T(1,128)S(1)}, f32[49,1,128]{2,1,0:T(1,128)S(1)}, u32[]{:S(2)}, u32[]{:S(2)}) collective-permute-start(f32[49,1,128]{2,1,0:T(1,128)S(1)} %get-tuple-element.298), channel_id=1, source_target_pairs={{0,4},{4,8},{8,12},{12,0},{1,5},{5,9},{9,13},{13,1},{2,6},{6,10},{... | collective-permute-start | bytes 75272 | tf_op jit(solution)/shard_map/ppermute | solution.py:23
  80.0 1.8 %collective-permute-done.13 = f32[49,1,128]{2,1,0:T(1,128)S(1)} collective-permute-done((f32[49,1,128]{2,1,0:T(1,128)S(1)}, f32[49,1,128]{2,1,0:T(1,128)S(1)}, u32[]{:S(2)}, u32[]{:S(2)}) %collective-permute-start.13) | collective-permute-done | bytes 25120 | tf_op jit(solution)/shard_map/ppermute | solution.py:25
  81.8 1.9 %collective-permute-done.12 = f32[49,1,128]{2,1,0:T(1,128)S(1)} collective-permute-done((f32[49,1,128]{2,1,0:T(1,128)S(1)}, f32[49,1,128]{2,1,0:T(1,128)S(1)}, u32[]{:S(2)}, u32[]{:S(2)}) %collective-permute-start.12) | collective-permute-done | bytes 25120 | tf_op jit(solution)/shard_map/ppermute | solution.py:23
  84.6 8.8 %collective-permute-done.15 = f32[49,10,1]{2,1,0:T(8,128)S(1)} collective-permute-done((f32[49,10,1]{2,1,0:T(8,128)S(1)}, f32[49,10,1]{2,1,0:T(8,128)S(1)}, u32[]{:S(2)}, u32[]{:S(2)}) %collective-permute-start.15) | collective-permute-done | bytes 1992 | tf_op jit(solution)/shard_map/ppermute | solution.py:25
  98.5 3.4 %collective-permute-done.16 = f32[49,128]{1,0:T(8,128)S(1)} collective-permute-done((f32[49,128]{1,0:T(8,128)S(1)}, f32[49,128]{1,0:T(8,128)S(1)}, u32[]{:S(2)}, u32[]{:S(2)}) %collective-permute-start.16) | collective-permute-done | bytes 25120 | tf_op jit(solution)/shard_map/ppermute | solution.py:35
  103.7 3.0 %collective-permute-start.19 = (f32[49,8]{0,1:T(8,128)S(1)}, f32[49,8]{0,1:T(8,128)S(1)}, u32[]{:S(2)}, u32[]{:S(2)}) collective-permute-start(f32[49,8]{0,1:T(8,128)S(1)} %get-tuple-element.206), channel_id=1, source_target_pairs={{0,1},{1,2},{2,3},{4,5},{5,6},{6,7},{8,9},{9,10},{10,11},{12,13},{... | collective-permute-start | bytes 4712 | tf_op jit(solution)/shard_map/ppermute | solution.py:41
  112.2 3.8 %collective-permute-start.20 = (f32[49,128]{1,0:T(8,128)S(1)}, f32[49,128]{1,0:T(8,128)S(1)}, u32[]{:S(2)}, u32[]{:S(2)}) collective-permute-start(f32[49,128]{1,0:T(8,128)S(1)} %bitcast.164), channel_id=1, source_target_pairs={{4,0},{8,4},{12,8},{0,12},{5,1},{9,5},{13,9},{1,13},{6,2},{10,6},{... | collective-permute-start | bytes 75272 | tf_op jit(solution)/shard_map/ppermute | solution.py:35
  117.7 3.0 %collective-permute-start.23 = (f32[49,8]{0,1:T(8,128)S(1)}, f32[49,8]{0,1:T(8,128)S(1)}, u32[]{:S(2)}, u32[]{:S(2)}) collective-permute-start(f32[49,8]{0,1:T(8,128)S(1)} %bitcast.177), channel_id=1, source_target_pairs={{0,1},{1,2},{2,3},{4,5},{5,6},{6,7},{8,9},{9,10},{10,11},{12,13},{... | collective-permute-start | bytes 4712 | tf_op jit(solution)/shard_map/ppermute | solution.py:41
  121.9 4.8 %collective-permute-done.21 = f32[49,128]{1,0:T(8,128)S(1)} collective-permute-done((f32[49,128]{1,0:T(8,128)S(1)}, f32[49,128]{1,0:T(8,128)S(1)}, u32[]{:S(2)}, u32[]{:S(2)}) %collective-permute-start.21) | collective-permute-done | bytes 25120 | tf_op jit(solution)/shard_map/ppermute | solution.py:35
  127.0 3.6 %scatter-add.64 = f32[49,8,128]{2,1,0:T(8,128)S(1)} dynamic-update-slice(f32[49,8,128]{2,1,0:T(8,128)S(1)} %scatter-add.61, f32[49,8,1]{2,1,0:T(8,128)S(1)} %slice_add_fusion.7, s32[]{:T(128)} %constant.418.clone.1, s32[]{:T(128)} %constant.418.clone.1, s32[]{:T(128)} %constant.433.clone.1) | dynamic-update-slice | bytes 3140 | tf_op jit(solution)/shard_map/scatter-add | solution.py:124
  135.6 3.9 %collective-permute-start.27 = (f32[49,8]{0,1:T(8,128)S(1)}, f32[49,8]{0,1:T(8,128)S(1)}, u32[]{:S(2)}, u32[]{:S(2)}) collective-permute-start(f32[49,8]{0,1:T(8,128)S(1)} %bitcast.179), channel_id=1, source_target_pairs={{0,1},{1,2},{2,3},{4,5},{5,6},{6,7},{8,9},{9,10},{10,11},{12,13},{... | collective-permute-start | bytes 4712 | tf_op jit(solution)/shard_map/ppermute | solution.py:41
  142.1 3.3 %collective-permute-done.25 = f32[49,128]{1,0:T(8,128)S(1)} collective-permute-done((f32[49,128]{1,0:T(8,128)S(1)}, f32[49,128]{1,0:T(8,128)S(1)}, u32[]{:S(2)}, u32[]{:S(2)}) %collective-permute-start.25) | collective-permute-done | bytes 25120 | tf_op jit(solution)/shard_map/ppermute | solution.py:35
  145.7 3.6 %scatter-add.70 = f32[49,8,128]{2,1,0:T(8,128)S(1)} dynamic-update-slice(f32[49,8,128]{2,1,0:T(8,128)S(1)} %scatter-add.69, f32[49,8,1]{2,1,0:T(8,128)S(1)} %slice_add_fusion.5, s32[]{:T(128)} %constant.418.clone.1, s32[]{:T(128)} %constant.418.clone.1, s32[]{:T(128)} %constant.433.clone.1) | dynamic-update-slice | bytes 3140 | tf_op jit(solution)/shard_map/scatter-add | solution.py:124
  154.5 3.1 %collective-permute-start.31 = (f32[49,8]{0,1:T(8,128)S(1)}, f32[49,8]{0,1:T(8,128)S(1)}, u32[]{:S(2)}, u32[]{:S(2)}) collective-permute-start(f32[49,8]{0,1:T(8,128)S(1)} %get-tuple-element.204), channel_id=1, source_target_pairs={{0,1},{1,2},{2,3},{4,5},{5,6},{6,7},{8,9},{9,10},{10,11},{12,13},{... | collective-permute-start | bytes 4712 | tf_op jit(solution)/shard_map/ppermute | solution.py:41
  157.8 2.0 %collective-permute-start.29 = (f32[49,128]{1,0:T(8,128)S(1)}, f32[49,128]{1,0:T(8,128)S(1)}, u32[]{:S(2)}, u32[]{:S(2)}) collective-permute-start(f32[49,128]{1,0:T(8,128)S(1)} %get-tuple-element.228), channel_id=1, source_target_pairs={{12,0},{0,4},{4,8},{8,12},{13,1},{1,5},{5,9},{9,13},{14,2},{2,6},{... | collective-permute-start | bytes 75272 | tf_op jit(solution)/shard_map/ppermute | solution.py:35
  160.2 3.3 %collective-permute-done.29 = f32[49,128]{1,0:T(8,128)S(1)} collective-permute-done((f32[49,128]{1,0:T(8,128)S(1)}, f32[49,128]{1,0:T(8,128)S(1)}, u32[]{:S(2)}, u32[]{:S(2)}) %collective-permute-start.29) | collective-permute-done | bytes 25120 | tf_op jit(solution)/shard_map/ppermute | solution.py:35
  (215 shorter events, 46.1 us)
Async XLA Ops:
  2.4 14.0 %all-to-all-start = ((f32[1,1,4,12288]{3,1,0,2:T(1,128)}), f32[1,1,4,12288]{3,1,0,2:T(1,128)S(1)}, u32[]{:S(2)}, u32[]{:S(2)}) async-start(f32[1,1,4,12288]{3,1,0,2:T(1,128)} %copy.263), calls=%async_computation | async-start | bytes 393216 | tf_op jit(solution)/shard_map/all_to_all | solution.py:81
  18.1 3.9 %collective-permute-start.1 = (f32[49,1,128]{2,1,0:T(1,128)S(1)}, f32[49,1,128]{2,1,0:T(1,128)S(1)}, u32[]{:S(2)}, u32[]{:S(2)}) collective-permute-start(f32[49,1,128]{2,1,0:T(1,128)S(1)} %get-tuple-element.305), channel_id=1, source_target_pairs={{4,0},{8,4},{12,8},{0,12},{5,1},{9,5},{13,9},{1,13},{6,2},{10,6},{... | collective-permute-start | bytes 75272 | tf_op jit(solution)/shard_map/ppermute | solution.py:25
  19.5 5.6 %collective-permute-start = (f32[49,1,128]{2,1,0:T(1,128)S(1)}, f32[49,1,128]{2,1,0:T(1,128)S(1)}, u32[]{:S(2)}, u32[]{:S(2)}) collective-permute-start(f32[49,1,128]{2,1,0:T(1,128)S(1)} %get-tuple-element.304), channel_id=1, source_target_pairs={{0,4},{4,8},{8,12},{12,0},{1,5},{5,9},{9,13},{13,1},{2,6},{6,10},{... | collective-permute-start | bytes 75272 | tf_op jit(solution)/shard_map/ppermute | solution.py:23
  25.4 8.8 %collective-permute-start.3 = (f32[49,10,1]{2,1,0:T(8,128)S(1)}, f32[49,10,1]{2,1,0:T(8,128)S(1)}, u32[]{:S(2)}, u32[]{:S(2)}) collective-permute-start(f32[49,10,1]{2,1,0:T(8,128)S(1)} %get-tuple-element.239), channel_id=1, source_target_pairs={{1,0},{2,1},{3,2},{0,3},{5,4},{6,5},{7,6},{4,7},{9,8},{10,9},{11,1... | collective-permute-start | bytes 5888 | tf_op jit(solution)/shard_map/ppermute | solution.py:25
  25.5 11.6 %collective-permute-start.2 = (f32[49,10,1]{2,1,0:T(8,128)S(1)}, f32[49,10,1]{2,1,0:T(8,128)S(1)}, u32[]{:S(2)}, u32[]{:S(2)}) collective-permute-start(f32[49,10,1]{2,1,0:T(8,128)S(1)} %get-tuple-element.238), channel_id=1, source_target_pairs={{0,1},{1,2},{2,3},{3,0},{4,5},{5,6},{6,7},{7,4},{8,9},{9,10},{10,1... | collective-permute-start | bytes 5888 | tf_op jit(solution)/shard_map/ppermute | solution.py:23
  39.9 3.9 %collective-permute-start.5 = (f32[49,1,128]{2,1,0:T(1,128)S(1)}, f32[49,1,128]{2,1,0:T(1,128)S(1)}, u32[]{:S(2)}, u32[]{:S(2)}) collective-permute-start(f32[49,1,128]{2,1,0:T(1,128)S(1)} %get-tuple-element.303), channel_id=1, source_target_pairs={{4,0},{8,4},{12,8},{0,12},{5,1},{9,5},{13,9},{1,13},{6,2},{10,6},{... | collective-permute-start | bytes 75272 | tf_op jit(solution)/shard_map/ppermute | solution.py:25
  40.0 5.7 %collective-permute-start.4 = (f32[49,1,128]{2,1,0:T(1,128)S(1)}, f32[49,1,128]{2,1,0:T(1,128)S(1)}, u32[]{:S(2)}, u32[]{:S(2)}) collective-permute-start(f32[49,1,128]{2,1,0:T(1,128)S(1)} %get-tuple-element.302), channel_id=1, source_target_pairs={{0,4},{4,8},{8,12},{12,0},{1,5},{5,9},{9,13},{13,1},{2,6},{6,10},{... | collective-permute-start | bytes 75272 | tf_op jit(solution)/shard_map/ppermute | solution.py:23
  45.9 9.7 %collective-permute-start.7 = (f32[49,10,1]{2,1,0:T(8,128)S(1)}, f32[49,10,1]{2,1,0:T(8,128)S(1)}, u32[]{:S(2)}, u32[]{:S(2)}) collective-permute-start(f32[49,10,1]{2,1,0:T(8,128)S(1)} %get-tuple-element.237), channel_id=1, source_target_pairs={{1,0},{2,1},{3,2},{0,3},{5,4},{6,5},{7,6},{4,7},{9,8},{10,9},{11,1... | collective-permute-start | bytes 5888 | tf_op jit(solution)/shard_map/ppermute | solution.py:25
  46.0 10.7 %collective-permute-start.6 = (f32[49,10,1]{2,1,0:T(8,128)S(1)}, f32[49,10,1]{2,1,0:T(8,128)S(1)}, u32[]{:S(2)}, u32[]{:S(2)}) collective-permute-start(f32[49,10,1]{2,1,0:T(8,128)S(1)} %get-tuple-element.236), channel_id=1, source_target_pairs={{0,1},{1,2},{2,3},{3,0},{4,5},{5,6},{6,7},{7,4},{8,9},{9,10},{10,1... | collective-permute-start | bytes 5888 | tf_op jit(solution)/shard_map/ppermute | solution.py:23
  58.8 3.9 %collective-permute-start.9 = (f32[49,1,128]{2,1,0:T(1,128)S(1)}, f32[49,1,128]{2,1,0:T(1,128)S(1)}, u32[]{:S(2)}, u32[]{:S(2)}) collective-permute-start(f32[49,1,128]{2,1,0:T(1,128)S(1)} %get-tuple-element.301), channel_id=1, source_target_pairs={{4,0},{8,4},{12,8},{0,12},{5,1},{9,5},{13,9},{1,13},{6,2},{10,6},{... | collective-permute-start | bytes 75272 | tf_op jit(solution)/shard_map/ppermute | solution.py:25
  59.1 5.6 %collective-permute-start.8 = (f32[49,1,128]{2,1,0:T(1,128)S(1)}, f32[49,1,128]{2,1,0:T(1,128)S(1)}, u32[]{:S(2)}, u32[]{:S(2)}) collective-permute-start(f32[49,1,128]{2,1,0:T(1,128)S(1)} %get-tuple-element.300), channel_id=1, source_target_pairs={{0,4},{4,8},{8,12},{12,0},{1,5},{5,9},{9,13},{13,1},{2,6},{6,10},{... | collective-permute-start | bytes 75272 | tf_op jit(solution)/shard_map/ppermute | solution.py:23
  65.0 9.0 %collective-permute-start.11 = (f32[49,10,1]{2,1,0:T(8,128)S(1)}, f32[49,10,1]{2,1,0:T(8,128)S(1)}, u32[]{:S(2)}, u32[]{:S(2)}) collective-permute-start(f32[49,10,1]{2,1,0:T(8,128)S(1)} %get-tuple-element.235), channel_id=1, source_target_pairs={{1,0},{2,1},{3,2},{0,3},{5,4},{6,5},{7,6},{4,7},{9,8},{10,9},{11,1... | collective-permute-start | bytes 5888 | tf_op jit(solution)/shard_map/ppermute | solution.py:25
  65.1 11.4 %collective-permute-start.10 = (f32[49,10,1]{2,1,0:T(8,128)S(1)}, f32[49,10,1]{2,1,0:T(8,128)S(1)}, u32[]{:S(2)}, u32[]{:S(2)}) collective-permute-start(f32[49,10,1]{2,1,0:T(8,128)S(1)} %get-tuple-element.234), channel_id=1, source_target_pairs={{0,1},{1,2},{2,3},{3,0},{4,5},{5,6},{6,7},{7,4},{8,9},{9,10},{10,1... | collective-permute-start | bytes 5888 | tf_op jit(solution)/shard_map/ppermute | solution.py:23
  78.0 3.9 %collective-permute-start.13 = (f32[49,1,128]{2,1,0:T(1,128)S(1)}, f32[49,1,128]{2,1,0:T(1,128)S(1)}, u32[]{:S(2)}, u32[]{:S(2)}) collective-permute-start(f32[49,1,128]{2,1,0:T(1,128)S(1)} %get-tuple-element.299), channel_id=1, source_target_pairs={{4,0},{8,4},{12,8},{0,12},{5,1},{9,5},{13,9},{1,13},{6,2},{10,6},{... | collective-permute-start | bytes 75272 | tf_op jit(solution)/shard_map/ppermute | solution.py:25
  78.0 5.7 %collective-permute-start.12 = (f32[49,1,128]{2,1,0:T(1,128)S(1)}, f32[49,1,128]{2,1,0:T(1,128)S(1)}, u32[]{:S(2)}, u32[]{:S(2)}) collective-permute-start(f32[49,1,128]{2,1,0:T(1,128)S(1)} %get-tuple-element.298), channel_id=1, source_target_pairs={{0,4},{4,8},{8,12},{12,0},{1,5},{5,9},{9,13},{13,1},{2,6},{6,10},{... | collective-permute-start | bytes 75272 | tf_op jit(solution)/shard_map/ppermute | solution.py:23
  84.0 9.4 %collective-permute-start.15 = (f32[49,10,1]{2,1,0:T(8,128)S(1)}, f32[49,10,1]{2,1,0:T(8,128)S(1)}, u32[]{:S(2)}, u32[]{:S(2)}) collective-permute-start(f32[49,10,1]{2,1,0:T(8,128)S(1)} %get-tuple-element.233), channel_id=1, source_target_pairs={{1,0},{2,1},{3,2},{0,3},{5,4},{6,5},{7,6},{4,7},{9,8},{10,9},{11,1... | collective-permute-start | bytes 5888 | tf_op jit(solution)/shard_map/ppermute | solution.py:25
  84.0 11.0 %collective-permute-start.14 = (f32[49,10,1]{2,1,0:T(8,128)S(1)}, f32[49,10,1]{2,1,0:T(8,128)S(1)}, u32[]{:S(2)}, u32[]{:S(2)}) collective-permute-start(f32[49,10,1]{2,1,0:T(8,128)S(1)} %get-tuple-element.232), channel_id=1, source_target_pairs={{0,1},{1,2},{2,3},{3,0},{4,5},{5,6},{6,7},{7,4},{8,9},{9,10},{10,1... | collective-permute-start | bytes 5888 | tf_op jit(solution)/shard_map/ppermute | solution.py:23
  98.1 3.9 %collective-permute-start.16 = (f32[49,128]{1,0:T(8,128)S(1)}, f32[49,128]{1,0:T(8,128)S(1)}, u32[]{:S(2)}, u32[]{:S(2)}) collective-permute-start(f32[49,128]{1,0:T(8,128)S(1)} %fusion.36), channel_id=1, source_target_pairs={{4,0},{8,4},{12,8},{0,12},{5,1},{9,5},{13,9},{1,13},{6,2},{10,6},{... | collective-permute-start | bytes 75272 | tf_op jit(solution)/shard_map/ppermute | solution.py:35
  102.0 5.7 %collective-permute-start.17 = (f32[49,128]{1,0:T(8,128)S(1)}, f32[49,128]{1,0:T(8,128)S(1)}, u32[]{:S(2)}, u32[]{:S(2)}) collective-permute-start(f32[49,128]{1,0:T(8,128)S(1)} %get-tuple-element.230), channel_id=1, source_target_pairs={{12,0},{0,4},{4,8},{8,12},{13,1},{1,5},{5,9},{9,13},{14,2},{2,6},{... | collective-permute-start | bytes 75272 | tf_op jit(solution)/shard_map/ppermute | solution.py:35
  102.4 4.3 %collective-permute-start.18 = (f32[49,8]{0,1:T(8,128)S(1)}, f32[49,8]{0,1:T(8,128)S(1)}, u32[]{:S(2)}, u32[]{:S(2)}) collective-permute-start(f32[49,8]{0,1:T(8,128)S(1)} %get-tuple-element.207), channel_id=1, source_target_pairs={{1,0},{2,1},{3,2},{5,4},{6,5},{7,6},{9,8},{10,9},{11,10},{13,12},{... | collective-permute-start | bytes 4712 | tf_op jit(solution)/shard_map/ppermute | solution.py:41
  112.2 8.6 %collective-permute-start.20 = (f32[49,128]{1,0:T(8,128)S(1)}, f32[49,128]{1,0:T(8,128)S(1)}, u32[]{:S(2)}, u32[]{:S(2)}) collective-permute-start(f32[49,128]{1,0:T(8,128)S(1)} %bitcast.164), channel_id=1, source_target_pairs={{4,0},{8,4},{12,8},{0,12},{5,1},{9,5},{13,9},{1,13},{6,2},{10,6},{... | collective-permute-start | bytes 75272 | tf_op jit(solution)/shard_map/ppermute | solution.py:35
  116.3 4.9 %collective-permute-start.22 = (f32[49,8]{0,1:T(8,128)S(1)}, f32[49,8]{0,1:T(8,128)S(1)}, u32[]{:S(2)}, u32[]{:S(2)}) collective-permute-start(f32[49,8]{0,1:T(8,128)S(1)} %bitcast.173), channel_id=1, source_target_pairs={{1,0},{2,1},{3,2},{5,4},{6,5},{7,6},{9,8},{10,9},{11,10},{13,12},{... | collective-permute-start | bytes 4712 | tf_op jit(solution)/shard_map/ppermute | solution.py:41
  117.7 3.8 %collective-permute-start.23 = (f32[49,8]{0,1:T(8,128)S(1)}, f32[49,8]{0,1:T(8,128)S(1)}, u32[]{:S(2)}, u32[]{:S(2)}) collective-permute-start(f32[49,8]{0,1:T(8,128)S(1)} %bitcast.177), channel_id=1, source_target_pairs={{0,1},{1,2},{2,3},{4,5},{5,6},{6,7},{8,9},{9,10},{10,11},{12,13},{... | collective-permute-start | bytes 4712 | tf_op jit(solution)/shard_map/ppermute | solution.py:41
  121.0 5.7 %collective-permute-start.21 = (f32[49,128]{1,0:T(8,128)S(1)}, f32[49,128]{1,0:T(8,128)S(1)}, u32[]{:S(2)}, u32[]{:S(2)}) collective-permute-start(f32[49,128]{1,0:T(8,128)S(1)} %bitcast.162), channel_id=1, source_target_pairs={{12,0},{0,4},{4,8},{8,12},{13,1},{1,5},{5,9},{9,13},{14,2},{2,6},{... | collective-permute-start | bytes 75272 | tf_op jit(solution)/shard_map/ppermute | solution.py:35
  133.8 5.7 %collective-permute-start.24 = (f32[49,128]{1,0:T(8,128)S(1)}, f32[49,128]{1,0:T(8,128)S(1)}, u32[]{:S(2)}, u32[]{:S(2)}) collective-permute-start(f32[49,128]{1,0:T(8,128)S(1)} %bitcast.165), channel_id=1, source_target_pairs={{4,0},{8,4},{12,8},{0,12},{5,1},{9,5},{13,9},{1,13},{6,2},{10,6},{... | collective-permute-start | bytes 75272 | tf_op jit(solution)/shard_map/ppermute | solution.py:35
  134.2 7.5 %collective-permute-start.26 = (f32[49,8]{0,1:T(8,128)S(1)}, f32[49,8]{0,1:T(8,128)S(1)}, u32[]{:S(2)}, u32[]{:S(2)}) collective-permute-start(f32[49,8]{0,1:T(8,128)S(1)} %bitcast.175), channel_id=1, source_target_pairs={{1,0},{2,1},{3,2},{5,4},{6,5},{7,6},{9,8},{10,9},{11,10},{13,12},{... | collective-permute-start | bytes 4712 | tf_op jit(solution)/shard_map/ppermute | solution.py:41
  135.6 6.2 %collective-permute-start.27 = (f32[49,8]{0,1:T(8,128)S(1)}, f32[49,8]{0,1:T(8,128)S(1)}, u32[]{:S(2)}, u32[]{:S(2)}) collective-permute-start(f32[49,8]{0,1:T(8,128)S(1)} %bitcast.179), channel_id=1, source_target_pairs={{0,1},{1,2},{2,3},{4,5},{5,6},{6,7},{8,9},{9,10},{10,11},{12,13},{... | collective-permute-start | bytes 4712 | tf_op jit(solution)/shard_map/ppermute | solution.py:41
  139.7 5.7 %collective-permute-start.25 = (f32[49,128]{1,0:T(8,128)S(1)}, f32[49,128]{1,0:T(8,128)S(1)}, u32[]{:S(2)}, u32[]{:S(2)}) collective-permute-start(f32[49,128]{1,0:T(8,128)S(1)} %bitcast.160), channel_id=1, source_target_pairs={{12,0},{0,4},{4,8},{8,12},{13,1},{1,5},{5,9},{9,13},{14,2},{2,6},{... | collective-permute-start | bytes 75272 | tf_op jit(solution)/shard_map/ppermute | solution.py:35
  152.9 7.2 %collective-permute-start.28 = (f32[49,128]{1,0:T(8,128)S(1)}, f32[49,128]{1,0:T(8,128)S(1)}, u32[]{:S(2)}, u32[]{:S(2)}) collective-permute-start(f32[49,128]{1,0:T(8,128)S(1)} %get-tuple-element.229), channel_id=1, source_target_pairs={{4,0},{8,4},{12,8},{0,12},{5,1},{9,5},{13,9},{1,13},{6,2},{10,6},{... | collective-permute-start | bytes 75272 | tf_op jit(solution)/shard_map/ppermute | solution.py:35
  153.2 6.5 %collective-permute-start.30 = (f32[49,8]{0,1:T(8,128)S(1)}, f32[49,8]{0,1:T(8,128)S(1)}, u32[]{:S(2)}, u32[]{:S(2)}) collective-permute-start(f32[49,8]{0,1:T(8,128)S(1)} %get-tuple-element.205), channel_id=1, source_target_pairs={{1,0},{2,1},{3,2},{5,4},{6,5},{7,6},{9,8},{10,9},{11,10},{13,12},{... | collective-permute-start | bytes 4712 | tf_op jit(solution)/shard_map/ppermute | solution.py:41
  154.5 5.4 %collective-permute-start.31 = (f32[49,8]{0,1:T(8,128)S(1)}, f32[49,8]{0,1:T(8,128)S(1)}, u32[]{:S(2)}, u32[]{:S(2)}) collective-permute-start(f32[49,8]{0,1:T(8,128)S(1)} %get-tuple-element.204), channel_id=1, source_target_pairs={{0,1},{1,2},{2,3},{4,5},{5,6},{6,7},{8,9},{9,10},{10,11},{12,13},{... | collective-permute-start | bytes 4712 | tf_op jit(solution)/shard_map/ppermute | solution.py:41
  157.8 5.7 %collective-permute-start.29 = (f32[49,128]{1,0:T(8,128)S(1)}, f32[49,128]{1,0:T(8,128)S(1)}, u32[]{:S(2)}, u32[]{:S(2)}) collective-permute-start(f32[49,128]{1,0:T(8,128)S(1)} %get-tuple-element.228), channel_id=1, source_target_pairs={{12,0},{0,4},{4,8},{8,12},{13,1},{1,5},{5,9},{9,13},{14,2},{2,6},{... | collective-permute-start | bytes 75272 | tf_op jit(solution)/shard_map/ppermute | solution.py:35
  (14 other events, 18.8 us)
where the time goes:
time: 167 us; the launch traced here: 166 us
  waiting for transfers between devices  81.8 us (49%)
  starting transfers between devices  43.4 us (26%)
  local copies, waits for them, and re-layouts  27.1 us (16%)
  other arithmetic  12.1 us (7%)
  between operations  1.69 us (1%)
    ppermute x8, waiting for transfers between devices, padded_2(): lax.ppermute(head, axis, [((i + 1) % count, i) for i in range(count)])  41.7 us
    ppermute x8, starting transfers between devices, shifted_2(): lax.ppermute(value, axis, [(source, source + steps) for source in range(i...  18.3 us
    ppermute x8, waiting for transfers between devices, padded_2(): lax.ppermute(tail, axis, [(i, (i + 1) % count) for i in range(count)])  17 us
    ppermute x8, waiting for transfers between devices, shifted(): return lax.ppermute(block, axis, route)  14.8 us
    scatter-add x8, local copies, waits for them, and re-layouts, local(): summed = summed.at[:, :, -1].add(from_north).at[:, :, 0].add(from_south)  10.1 us
    ppermute x8, starting transfers between devices, padded_2(): lax.ppermute(tail, axis, [(i, (i + 1) % count) for i in range(count)])  8.42 us
    ppermute x8, starting transfers between devices, shifted(): return lax.ppermute(block, axis, route)  8.17 us
    unnamed x27, local copies, waits for them, and re-layouts  7.45 us
  transfers between devices with their start and end apart: 33, of which 23 were waited for; matrix products, arithmetic and copies ran while one was open for 3% of the time, Pallas kernels for 0%

commit v1 on v0

v1 whole, which is shorter than its diff:
```python
import functools
import jax
import jax.numpy as jnp
from jax import lax
from jax.experimental import pallas as pl
from jax.experimental.pallas import tpu as pltpu
from jax.sharding import PartitionSpec as P

ITERS = 4
ADVECTION = 0.3
VERTICAL_MIX = 0.1
HEIGHT_DIFFUSION = 0.2
HEIGHT_DAMPING = 0.3
BUOYANCY = 0.5

SUB = 8
LANE = 128
MESH = pl.DeviceIdType.MESH


def roll_lanes(value, shift):
    return pltpu.roll(value, shift, 1)


def roll_rows(value, shift):
    return pltpu.roll(value, shift, 0)


def kernel(
    n, n_y, levels, piece_rows,
    holder_ref, diff_ref, ckpt_ref, height_ref, mask_ref, tw_hbm, hw_ref,
    out_ref, outh_ref,
    buf, recv, state, dy, tw, lam, mu, wet, arow, brow, mrow, gurow, gvrow,
    packs, packr, slab_s, slab_r, bpacks, bpackr,
    a2a_send, a2a_recv, f_send, f_recv, b_send, b_recv, tw_sem,
):
    me = lax.axis_index("gx")
    my = lax.axis_index("gy")
    east, west = lax.rem(me + 1, n), lax.rem(me + n - 1, n)
    north, south = lax.rem(my + 1, n_y), lax.rem(my + n_y - 1, n_y)
    channels = 3 * levels
    tiles = channels // SUB
    per = levels // SUB
    hrow = channels
    padded = -(-piece_rows // SUB) * SUB

    tw_copy = pltpu.make_async_copy(tw_hbm, tw, tw_sem)
    tw_copy.start()

    barrier = pltpu.get_barrier_semaphore()
    for k in range(1, n):
        pl.semaphore_signal(barrier, inc=1, device_id={"gx": lax.rem(me + k, n)}, device_id_type=MESH)
    for other in (north, south):
        pl.semaphore_signal(barrier, inc=1, device_id={"gy": other}, device_id_type=MESH)

    depth = 0 if piece_rows % SUB else piece_rows // SUB
    if padded != piece_rows:
        buf[...] = jnp.zeros_like(buf)
    for o in range(0, n, SUB):
        size = min(SUB, n - o)
        for r in range(piece_rows):
            row = r % SUB * depth + r // SUB if depth else r
            buf[pl.ds(o * padded + row, size, stride=padded), :] = ckpt_ref[o:o + size, r * LANE:(r + 1) * LANE]

    pl.semaphore_wait(barrier, n + 1)

    mine = pl.multiple_of(me * padded, SUB)
    sends = []
    a2a = []
    for k in range(1, n):
        owner = lax.rem(me + k, n)
        copy = pltpu.make_async_remote_copy(
            src_ref=buf.at[pl.ds(pl.multiple_of(owner * padded, SUB), padded)],
            dst_ref=recv.at[me],
            send_sem=a2a_send.at[k], recv_sem=a2a_recv.at[k],
            device_id={"gx": owner}, device_id_type=MESH,
        )
        copy.start()
        a2a.append(copy)
    recv[me] = buf[pl.ds(mine, padded), :]

    lane = lax.broadcasted_iota(jnp.int32, (SUB, LANE), 1)
    sub = lax.broadcasted_iota(jnp.int32, (SUB, LANE), 0)
    first_lane, last_lane = lane == 0, lane == LANE - 1
    edge_lane = first_lane | last_lane
    first_row, last_row = sub == 0, sub == SUB - 1
    pair = lax.shift_right_logical(lane, 1)
    even = (lane & 1) == 0
    zero = jnp.zeros((SUB, LANE), jnp.float32)

    diff = []
    for t in range(tiles):
        value = zero
        for s in range(SUB):
            channel = t * SUB + s
            value = jnp.where(sub == s, diff_ref[channel // levels, channel % levels], value)
        diff.append(value)
    wet_tile = mask_ref[...].astype(jnp.float32)
    wet[...] = wet_tile
    for t in range(tiles):
        rows = pl.ds(t * SUB, SUB)
        mu[0, rows, :] = zero
        mu[SUB + 1, rows, :] = zero
    for t in range(ITERS):
        arow[t, 0:SUB, :] = zero
        arow[t, SUB:2 * SUB, :] = zero
    tw_copy.wait()
    for x in range(SUB):
        for t in range(tiles):
            lam[x, t * SUB:(t + 1) * SUB, :] = tw[pl.ds(t * SUB * SUB + x, SUB, stride=SUB), :]

    for copy in a2a:
        copy.wait_recv()
    for p in range(n):
        holder = holder_ref[0, 0, p]
        if depth:
            for x in range(SUB):
                state[0, x + 1, p * depth:(p + 1) * depth, :] = recv[holder, x * depth:(x + 1) * depth, :]
        else:
            for r in range(piece_rows):
                row = p * piece_rows + r
                state[0, row % SUB + 1, row // SUB:row // SUB + 1, :] = recv[holder, r:r + 1, :]

    def exchange(send_east, recv_east, send_west, recv_west, pack_out, pack_in, send_sem, recv_sem, step):
        route = (
            (send_east, recv_east, {"gx": east}),
            (send_west, recv_west, {"gx": west}),
            (pack_out, pack_in.at[step, 0], {"gy": north}),
            (pack_out, pack_in.at[step, 1], {"gy": south}),
        )
        copies = []
        for i, (source, target, device) in enumerate(route):
            copy = pltpu.make_async_remote_copy(
                src_ref=source, dst_ref=target, send_sem=send_sem.at[step, i], recv_sem=recv_sem.at[step, i],
                device_id=device, device_id_type=MESH,
            )
            copy.start()
            copies.append(copy)
        sends.extend(copies)
        return copies

    def unpacked(pack_in, step):
        from_south = jnp.where(my > 0, roll_lanes(pack_in[step, 0], 1), zero)
        from_north = jnp.where(my < n_y - 1, roll_lanes(pack_in[step, 1], LANE - 1), zero)
        return jnp.where(even, from_north, from_south)

    def spread(columns, k):
        return roll_lanes(columns, lax.rem(2 * LANE - 1 - 2 * k, LANE))

    def packed_with(packed, value, k):
        return jnp.where(pair == k, roll_lanes(value, 2 * k + 1), packed)

    def vertical(values):
        result = [None] * tiles
        for tracer in range(3):
            group = values[tracer * per:(tracer + 1) * per]
            down = [roll_rows(v, 1) for v in group]
            up = [roll_rows(v, SUB - 1) for v in group]
            for i, v in enumerate(group):
                upper = jnp.where(first_row, down[i - 1] if i else v, down[i])
                lower = jnp.where(last_row, up[i + 1] if i < per - 1 else v, up[i])
                result[tracer * per + i] = upper + lower - 2.0 * v
        return result

    def row_of(ref, x):
        return jnp.broadcast_to(ref[pl.ds(x, 1), :], (SUB, LANE))

    def send_state(step, packed, h):
        packs[step] = packed_with(packed, h, channels)
        state[step, 1, hrow:hrow + SUB, :] = jnp.broadcast_to(h[0:1, :], (SUB, LANE))
        state[step, SUB, hrow:hrow + SUB, :] = jnp.broadcast_to(h[SUB - 1:SUB, :], (SUB, LANE))
        return exchange(
            state.at[step, SUB], state.at[step, 0], state.at[step, 1], state.at[step, SUB + 1],
            packs.at[step], packr, f_send, f_recv, step,
        )

    hslot = channels

    def pack_body(x, packed):
        for t in range(tiles):
            packed = packed_with(packed, state[0, x + 1, t * SUB:(t + 1) * SUB, :], x * tiles + t)
        return packed

    heights = [height_ref[...]]
    copies = send_state(0, lax.fori_loop(0, SUB, pack_body, zero), heights[0])

    for step in range(ITERS):
        h = heights[step]
        final = step == ITERS - 1
        damp = jnp.tanh(h)
        for copy in copies:
            copy.wait_recv()
        columns = unpacked(packr, step)
        side = spread(columns, hslot)
        h_w = jnp.where(first_row, jnp.broadcast_to(state[step, 0, hrow:hrow + 1, :], (SUB, LANE)), roll_rows(h, 1))
        h_e = jnp.where(last_row, jnp.broadcast_to(state[step, SUB + 1, hrow:hrow + 1, :], (SUB, LANE)), roll_rows(h, SUB - 1))
        h_s = jnp.where(first_lane, side, roll_lanes(h, 1))
        h_n = jnp.where(last_lane, side, roll_lanes(h, LANE - 1))
        arow[step, 1:SUB + 1, :] = (-0.25 * ADVECTION) * (h_n - h_s)
        brow[step] = (0.25 * ADVECTION) * (h_e - h_w)

        def forward_body(x, packed):
            a = row_of(arow.at[step], x + 1)
            b = row_of(brow.at[step], x)
            w = row_of(wet, x)
            centre = [state[step, x + 1, t * SUB:(t + 1) * SUB, :] for t in range(tiles)]
            if not final:
                vert = vertical(centre)
                total = centre[0]
                for i in range(1, per):
                    total = total + centre[i]
                mrow[pl.ds(x, 1), :] = jnp.sum(total, axis=0, keepdims=True)
            for t in range(tiles):
                rows = slice(t * SUB, (t + 1) * SUB)
                c = centre[t]
                side = spread(columns, x * tiles + t)
                c_s = jnp.where(first_lane, side, roll_lanes(c, 1))
                c_n = jnp.where(last_lane, side, roll_lanes(c, LANE - 1))
                delta = c_n - c_s
                dy[step, x, rows, :] = delta
                if not final:
                    c_e = state[step, x + 2, rows, :]
                    c_w = state[step, x, rows, :]
                    lap = c_e + c_w + c_n + c_s - 4.0 * c
                    new = c + w * (diff[t] * lap - a * (c_e - c_w) - b * delta + VERTICAL_MIX * vert[t])
                    state[step + 1, x + 1, rows, :] = new
                    packed = packed_with(packed, new, x * tiles + t)
            return packed

        packed = lax.fori_loop(0, SUB, forward_body, zero)
        if not final:
            lap = h_e + h_w + h_n + h_s - 4.0 * h
            h = h + HEIGHT_DIFFUSION * lap - HEIGHT_DAMPING * damp + (BUOYANCY / levels) * wet_tile * mrow[...]
            heights.append(h)
            copies = send_state(step + 1, packed, h)

    lam_h = hw_ref[...]
    columns = None
    for step in reversed(range(ITERS)):

        def gather_body(x, packed):
            b = row_of(brow.at[step], x)
            w = row_of(wet, x)
            gu = zero
            gv = zero
            for t in range(tiles):
                rows = slice(t * SUB, (t + 1) * SUB)
                value = lam[x, rows, :]
                if columns is not None:
                    value = value + jnp.where(edge_lane, spread(columns, x * tiles + t), 0.0)
                    lam[x, rows, :] = value
                m = w * value
                mu[x + 1, rows, :] = m
                bm = b * m
                dm = diff[t] * m
                packed = packed_with(packed, jnp.where(last_lane, dm - bm, dm + bm), x * tiles + t)
                gu = gu + m * (state[step, x + 2, rows, :] - state[step, x, rows, :])
                gv = gv + m * dy[step, x, rows, :]
            gurow[pl.ds(x, 1), :] = jnp.sum(gu, axis=0, keepdims=True)
            gvrow[pl.ds(x, 1), :] = jnp.sum(gv, axis=0, keepdims=True)
            return packed

        packed = lax.fori_loop(0, SUB, gather_body, zero)
        gu = (-0.25 * ADVECTION) * gurow[...]
        gv = (-0.25 * ADVECTION) * gvrow[...]
        spread_h = HEIGHT_DIFFUSION * lam_h
        to_e, to_w, to_n, to_s = spread_h + gv, spread_h - gv, spread_h - gu, spread_h + gu
        bpacks[step] = packed_with(packed, jnp.where(last_lane, to_n, to_s), hslot)
        a_last = row_of(arow.at[step], SUB)
        a_first = row_of(arow.at[step], 1)
        for t in range(tiles):
            rows = slice(t * SUB, (t + 1) * SUB)
            slab_s[step, 0, rows, :] = (diff[t] - a_last) * mu[SUB, rows, :]
            slab_s[step, 1, rows, :] = (diff[t] + a_first) * mu[1, rows, :]
        slab_s[step, 0, hrow:hrow + SUB, :] = jnp.broadcast_to(to_e[SUB - 1:SUB, :], (SUB, LANE))
        slab_s[step, 1, hrow:hrow + SUB, :] = jnp.broadcast_to(to_w[0:1, :], (SUB, LANE))
        copies = exchange(
            slab_s.at[step, 0], slab_r.at[step, 0], slab_s.at[step, 1], slab_r.at[step, 1],
            bpacks.at[step], bpackr, b_send, b_recv, step,
        )

        source = (BUOYANCY / levels) * wet_tile * lam_h
        mrow[...] = source

        def local_body(x, carry):
            a_w = row_of(arow.at[step], x)
            a_e = row_of(arow.at[step], x + 2)
            b = row_of(brow.at[step], x)
            centre = [mu[x + 1, t * SUB:(t + 1) * SUB, :] for t in range(tiles)]
            vert = vertical(centre)
            push = row_of(mrow, x)
            for t in range(tiles):
                rows = slice(t * SUB, (t + 1) * SUB)
                m = centre[t]
                m_w = mu[x, rows, :]
                m_e = mu[x + 2, rows, :]
                bm = b * m
                dm = diff[t] * m
                from_s = jnp.where(first_lane, 0.0, roll_lanes(dm - bm, 1))
                from_n = jnp.where(last_lane, 0.0, roll_lanes(dm + bm, LANE - 1))
                value = lam[x, rows, :] + VERTICAL_MIX * vert[t] - 4.0 * dm + from_s + from_n
                value = value + diff[t] * (m_w + m_e) + (a_e * m_e - a_w * m_w)
                if t < per:
                    value = value + push
                lam[x, rows, :] = value
            return carry

        lax.fori_loop(0, SUB, local_body, 0)
        damp = jnp.tanh(heights[step])
        lam_h = (
            lam_h - 4.0 * spread_h - HEIGHT_DAMPING * (1.0 - damp * damp) * lam_h
            + jnp.where(first_row, 0.0, roll_rows(to_e, 1)) + jnp.where(last_row, 0.0, roll_rows(to_w, SUB - 1))
            + jnp.where(first_lane, 0.0, roll_lanes(to_n, 1)) + jnp.where(last_lane, 0.0, roll_lanes(to_s, LANE - 1))
        )
        for copy in copies:
            copy.wait_recv()
        columns = unpacked(bpackr, step)
        for t in range(tiles):
            rows = slice(t * SUB, (t + 1) * SUB)
            lam[0, rows, :] = lam[0, rows, :] + slab_r[step, 0, rows, :]
            lam[SUB - 1, rows, :] = lam[SUB - 1, rows, :] + slab_r[step, 1, rows, :]
        lam_h = lam_h + jnp.where(edge_lane, spread(columns, hslot), 0.0)
        lam_h = lam_h + jnp.where(first_row, jnp.broadcast_to(slab_r[step, 0, hrow:hrow + 1, :], (SUB, LANE)), 0.0)
        lam_h = lam_h + jnp.where(last_row, jnp.broadcast_to(slab_r[step, 1, hrow:hrow + 1, :], (SUB, LANE)), 0.0)

    outh_ref[...] = lam_h
    for x in range(SUB):
        for t in range(tiles):
            value = lam[x, t * SUB:(t + 1) * SUB, :] + jnp.where(edge_lane, spread(columns, x * tiles + t), 0.0)
            out_ref[pl.ds(t * SUB * SUB + x, SUB, stride=SUB), :] = value

    for copy in a2a + sends:
        copy.wait_send()


def local(checkpoint, holder_list, height, land_mask, diffusivity, tracer_weight, height_weight):
    n, n_y = lax.axis_size("gx"), lax.axis_size("gy")
    width_x, width_y = height.shape
    assert (width_x, width_y) == (SUB, LANE)
    levels = diffusivity.shape[1]
    channels = 3 * levels
    piece_rows = checkpoint.shape[3] // LANE
    padded = -(-piece_rows // SUB) * SUB
    rows = channels + SUB
    f32 = jnp.float32
    vmem = pl.BlockSpec(memory_space=pltpu.VMEM)
    smem = pl.BlockSpec(memory_space=pltpu.SMEM)
    tile = pltpu.VMEM((SUB, LANE), f32)
    out, out_h = pl.pallas_call(
        functools.partial(kernel, n, n_y, levels, piece_rows),
        out_shape=(
            jax.ShapeDtypeStruct((channels * SUB, LANE), f32),
            jax.ShapeDtypeStruct((SUB, LANE), f32),
        ),
        in_specs=[smem, smem, vmem, vmem, vmem, pl.BlockSpec(memory_space=pl.ANY), vmem],
        out_specs=(vmem, vmem),
        scratch_shapes=[
            pltpu.VMEM((n * padded, LANE), f32),
            pltpu.VMEM((n, padded, LANE), f32),
            pltpu.VMEM((ITERS, SUB + 2, rows, LANE), f32),
            pltpu.VMEM((ITERS, SUB, channels, LANE), f32),
            pltpu.VMEM((channels * SUB, LANE), f32),
            pltpu.VMEM((SUB, channels, LANE), f32),
            pltpu.VMEM((SUB + 2, channels, LANE), f32),
            tile,
            pltpu.VMEM((ITERS, 2 * SUB, LANE), f32),
            pltpu.VMEM((ITERS, SUB, LANE), f32),
            tile, tile, tile,
            pltpu.VMEM((ITERS, SUB, LANE), f32),
            pltpu.VMEM((ITERS, 2, SUB, LANE), f32),
            pltpu.VMEM((ITERS, 2, rows, LANE), f32),
            pltpu.VMEM((ITERS, 2, rows, LANE), f32),
            pltpu.VMEM((ITERS, SUB, LANE), f32),
            pltpu.VMEM((ITERS, 2, SUB, LANE), f32),
            pltpu.SemaphoreType.DMA((n,)),
            pltpu.SemaphoreType.DMA((n,)),
            pltpu.SemaphoreType.DMA((ITERS, 4)),
            pltpu.SemaphoreType.DMA((ITERS, 4)),
            pltpu.SemaphoreType.DMA((ITERS, 4)),
            pltpu.SemaphoreType.DMA((ITERS, 4)),
            pltpu.SemaphoreType.DMA,
        ],
        compiler_params=pltpu.CompilerParams(
            collective_id=0, has_side_effects=True, vmem_limit_bytes=32 * 2**20
        ),
    )(
        holder_list, diffusivity, checkpoint.reshape(checkpoint.shape[2:]), height, land_mask,
        tracer_weight.reshape(channels * SUB, LANE), height_weight,
    )
    return out.reshape(tracer_weight.shape), out_h


def solution(mesh):
    return jax.shard_map(
        local,
        mesh=mesh,
        in_specs=(
            P(("member", "gx"), "gy", None, None),
            P(("member", "gx"), "gy", None),
            P(("member", "gx"), "gy"),
            P("gx", "gy"),
            P(),
            P("member", None, "gx", "gy"),
            P(("member", "gx"), "gy"),
        ),
        out_specs=(P("member", None, "gx", "gy"), P(("member", "gx"), "gy")),
        check_vma=False,
    )
```

time: 167 us -> 60.8 us (0.36)
  waiting for transfers between devices: 81.8 us -> 0 us
  Pallas kernels: 0 us -> 54 us
  starting transfers between devices: 43.4 us -> 0 us
  local copies, waits for them, and re-layouts: 27.1 us -> 5.85 us
  other arithmetic: 12.1 us -> 0 us
    ppermute x32 -> x0, waiting for transfers between devices: 74.4 us -> none  [the longest x8 41.7 us: padded_2(): lax.ppermute(head, axis, [((i + 1) % count, i) for i in range(count)])]
    pallas_call x0 -> x1, Pallas kernels: none -> 54 us  [local(): pl.pallas_call(functools.partial(kernel, n, n_y, levels, piece_rows), out...]
    ppermute x32 -> x0, starting transfers between devices: 37 us -> none  [the longest x8 18.3 us: shifted_2(): lax.ppermute(value, axis, [(source, source + steps) for source in range(i...]
    scatter-add x12 -> x0, local copies, waits for them, and re-layouts: 10.6 us -> none  [the longest x8 10.1 us: local(): summed = summed.at[:, :, -1].add(from_north).at[:, :, 0].add(from_south)]
    all_to_all x1 -> x0, waiting for transfers between devices: 7.32 us -> none  [local(): lax.all_to_all(checkpoint, 'gx', split_axis=2, concat_axis=0, tiled=True)]
    all_to_all x1 -> x0, starting transfers between devices: 6.45 us -> none  [local(): lax.all_to_all(checkpoint, 'gx', split_axis=2, concat_axis=0, tiled=True)]
    slice x28 -> x0, local copies, waits for them, and re-layouts: 4.1 us -> none  [the longest x6 0.86 us: local(): adjoint_tracers = summed[:channels].reshape(3, levels, width_x, width_y)]
    add_any x7 -> x0, other arithmetic: 3.39 us -> none  [the longest x4 3.14 us: advance(): east_cell = tracer_pad[..., 2:, 1:-1]]
  transfers between devices with their start and end apart: 33 -> 0, of which waited for: 23 -> 0; matrix products, arithmetic and copies ran while one was open for 3% -> 0% of each run, Pallas kernels for 0% -> 0%
where the time goes in v1:
time: 60.8 us; the launch traced here: 60.5 us
  Pallas kernels  54 us (89%)
  local copies, waits for them, and re-layouts  5.85 us (10%)
  between operations  0.66 us (1%)
    pallas_call x1, Pallas kernels, local(): pl.pallas_call(functools.partial(kernel, n, n_y, levels, piece_rows), out...  54 us
    unnamed x16, local copies, waits for them, and re-layouts  5.85 us

profile of v1, /device:TPU:0, one launch (start us, length us, event | category | flops | bytes accessed | tf_op | source)
XLA Modules:
  0.0 60.5 jit_solution(325924015372658440)
XLA Ops:
  0.6 0.0 copy-start.5
  0.6 0.0 copy-start.6
  0.7 0.7 %copy-done.5 = f32[3,16]{1,0:T(4,128)S(1)} copy-done((f32[3,16]{1,0:T(4,128)S(1)}, f32[3,16]{1,0:T(4,128)}, u32[]{:S(2)}) %copy-start.5) | copy-done | bytes 216
  1.3 0.0 copy-done.6
  1.3 0.0 copy-start
  1.3 0.9 %copy-done = f32[1,1,4,12288]{3,2,1,0:T(4,128)S(1)} copy-done((f32[1,1,4,12288]{3,2,1,0:T(4,128)S(1)}, f32[1,1,4,12288]{3,2,1,0:T(4,128)}, u32[]{:S(2)}) %copy-start) | copy-done | bytes 196632
  2.2 0.0 copy-start.1
  2.2 0.9 %copy-done.1 = f32[3,16,8,128]{3,2,1,0:T(8,128)S(1)} copy-done((f32[3,16,8,128]{3,2,1,0:T(8,128)S(1)}, f32[3,16,8,128]{3,2,1,0:T(8,128)}, u32[]{:S(2)}) %copy-start.1) | copy-done | bytes 196632
  3.2 0.0 copy-start.2
  3.2 0.7 %copy-done.2 = f32[8,128]{1,0:T(8,128)S(1)} copy-done((f32[8,128]{1,0:T(8,128)S(1)}, f32[8,128]{1,0:T(8,128)}, u32[]{:S(2)}) %copy-start.2) | copy-done | bytes 4120
  3.9 0.0 copy-start.3
  3.9 0.7 %copy-done.3 = s32[8,128]{1,0:T(8,128)S(1)} copy-done((s32[8,128]{1,0:T(8,128)S(1)}, s32[8,128]{1,0:T(8,128)}, u32[]{:S(2)}) %copy-start.3) | copy-done | bytes 4120
  4.5 0.0 copy-start.4
  4.5 0.7 %copy-done.4 = f32[8,128]{1,0:T(8,128)S(1)} copy-done((f32[8,128]{1,0:T(8,128)S(1)}, f32[8,128]{1,0:T(8,128)}, u32[]{:S(2)}) %copy-start.4) | copy-done | bytes 4120
  5.2 54.0 %shard_map.86 = (f32[384,128]{1,0:T(8,128)S(1)}, f32[8,128]{1,0:T(8,128)S(1)}) custom-call(s32[1,1,4]{2,1,0:T(1,128)S(1)} %copy-done.6, f32[3,16]{1,0:T(4,128)S(1)} %copy-done.5, f32[4,12288]{1,0:T(4,128)S(1)} %bitcast.3, f32[8,128]{1,0:T(8,128)S(1)} %copy-done.2, s32[8,128]{1,0:T(8,128)S(1)} %copy-done.3, f32[384,128]{1,0:T(8,128)S(1)} %bitcast.4, ...), custom_call_target="tpu_custom_call" | custom-call | tf_op jit(solution)/shard_map/pallas_call | solution.py:349
  59.2 0.7 %copy.11 = f32[3,16,8,128]{3,2,1,0:T(8,128)} copy(f32[3,16,8,128]{3,2,1,0:T(8,128)S(1)} %bitcast.5) | data formatting | bytes 393216
  59.9 0.6 copy.12
Async XLA Ops:
  0.6 0.7 %copy-start.5 = (f32[3,16]{1,0:T(4,128)S(1)}, f32[3,16]{1,0:T(4,128)}, u32[]{:S(2)}) copy-start(f32[3,16]{1,0:T(4,128)} %diff_ref.1) | copy-start | bytes 580
  0.6 0.7 %copy-start.6 = (s32[1,1,4]{2,1,0:T(1,128)S(1)}, s32[1,1,4]{2,1,0:T(1,128)}, u32[]{:S(2)}) copy-start(s32[1,1,4]{2,1,0:T(1,128)} %holder_ref.1) | copy-start | bytes 52
  1.3 0.9 %copy-start = (f32[1,1,4,12288]{3,2,1,0:T(4,128)S(1)}, f32[1,1,4,12288]{3,2,1,0:T(4,128)}, u32[]{:S(2)}) copy-start(f32[1,1,4,12288]{3,2,1,0:T(4,128)} %param.7) | copy-start | bytes 589828
  2.2 0.9 %copy-start.1 = (f32[3,16,8,128]{3,2,1,0:T(8,128)S(1)}, f32[3,16,8,128]{3,2,1,0:T(8,128)}, u32[]{:S(2)}) copy-start(f32[3,16,8,128]{3,2,1,0:T(8,128)} %param.12) | copy-start | bytes 589828
  3.2 0.7 %copy-start.2 = (f32[8,128]{1,0:T(8,128)S(1)}, f32[8,128]{1,0:T(8,128)}, u32[]{:S(2)}) copy-start(f32[8,128]{1,0:T(8,128)} %height_ref.1) | copy-start | bytes 12292
  3.9 0.7 %copy-start.3 = (s32[8,128]{1,0:T(8,128)S(1)}, s32[8,128]{1,0:T(8,128)}, u32[]{:S(2)}) copy-start(s32[8,128]{1,0:T(8,128)} %mask_ref.1) | copy-start | bytes 12292
  4.5 0.7 %copy-start.4 = (f32[8,128]{1,0:T(8,128)S(1)}, f32[8,128]{1,0:T(8,128)}, u32[]{:S(2)}) copy-start(f32[8,128]{1,0:T(8,128)} %hw_ref.1) | copy-start | bytes 12292

commit v2 on v1

--- a/solution.py
+++ b/solution.py
@@ -28,11 +28,12 @@
 
 def kernel(
     n, n_y, levels, piece_rows,
-    holder_ref, diff_ref, ckpt_ref, height_ref, mask_ref, tw_hbm, hw_ref,
+    holder_hbm, diff_hbm, ckpt_hbm, height_hbm, mask_hbm, tw_hbm, hw_hbm,
     out_ref, outh_ref,
     buf, recv, state, dy, tw, lam, mu, wet, arow, brow, mrow, gurow, gvrow,
     packs, packr, slab_s, slab_r, bpacks, bpackr,
-    a2a_send, a2a_recv, f_send, f_recv, b_send, b_recv, tw_sem,
+    holder_ref, diff_ref, ckpt_ref, height_ref, mask_ref, hw_ref,
+    a2a_send, a2a_recv, f_send, f_recv, b_send, b_recv, in_sem,
 ):
     me = lax.axis_index("gx")
     my = lax.axis_index("gy")
@@ -44,8 +45,13 @@
     hrow = channels
     padded = -(-piece_rows // SUB) * SUB
 
-    tw_copy = pltpu.make_async_copy(tw_hbm, tw, tw_sem)
-    tw_copy.start()
+    inputs = (
+        (ckpt_hbm, ckpt_ref), (diff_hbm, diff_ref), (mask_hbm, mask_ref), (tw_hbm, tw),
+        (height_hbm, height_ref), (hw_hbm, hw_ref), (holder_hbm, holder_ref),
+    )
+    loads = [pltpu.make_async_copy(source, target, in_sem.at[i]) for i, (source, target) in enumerate(inputs)]
+    for load in loads:
+        load.start()
 
     barrier = pltpu.get_barrier_semaphore()
     for k in range(1, n):
@@ -53,6 +59,7 @@
     for other in (north, south):
         pl.semaphore_signal(barrier, inc=1, device_id={"gy": other}, device_id_type=MESH)
 
+    loads[0].wait()
     depth = 0 if piece_rows % SUB else piece_rows // SUB
     if padded != piece_rows:
         buf[...] = jnp.zeros_like(buf)
@@ -88,6 +95,9 @@
     even = (lane & 1) == 0
     zero = jnp.zeros((SUB, LANE), jnp.float32)
 
+    for load in loads[1:]:
+        load.wait()
+    mrow[...] = zero
     diff = []
     for t in range(tiles):
         value = zero
@@ -104,7 +114,6 @@
     for t in range(ITERS):
         arow[t, 0:SUB, :] = zero
         arow[t, SUB:2 * SUB, :] = zero
-    tw_copy.wait()
     for x in range(SUB):
         for t in range(tiles):
             lam[x, t * SUB:(t + 1) * SUB, :] = tw[pl.ds(t * SUB * SUB + x, SUB, stride=SUB), :]
@@ -121,15 +130,9 @@
                 row = p * piece_rows + r
                 state[0, row % SUB + 1, row // SUB:row // SUB + 1, :] = recv[holder, r:r + 1, :]
 
-    def exchange(send_east, recv_east, send_west, recv_west, pack_out, pack_in, send_sem, recv_sem, step):
-        route = (
-            (send_east, recv_east, {"gx": east}),
-            (send_west, recv_west, {"gx": west}),
-            (pack_out, pack_in.at[step, 0], {"gy": north}),
-            (pack_out, pack_in.at[step, 1], {"gy": south}),
-        )
+    def exchange(route, send_sem, recv_sem, step, first):
         copies = []
-        for i, (source, target, device) in enumerate(route):
+        for i, (source, target, device) in enumerate(route, first):
             copy = pltpu.make_async_remote_copy(
                 src_ref=source, dst_ref=target, send_sem=send_sem.at[step, i], recv_sem=recv_sem.at[step, i],
                 device_id=device, device_id_type=MESH,
@@ -138,6 +141,21 @@
             copies.append(copy)
         sends.extend(copies)
         return copies
+
+    def exchange_rows(send_east, recv_east, send_west, recv_west, send_sem, recv_sem, step):
+        route = ((send_east, recv_east, {"gx": east}), (send_west, recv_west, {"gx": west}))
+        return exchange(route, send_sem, recv_sem, step, 0)
+
+    def exchange_columns(pack_out, pack_in, send_sem, recv_sem, step):
+        route = ((pack_out, pack_in.at[step, 0], {"gy": north}), (pack_out, pack_in.at[step, 1], {"gy": south}))
+        return exchange(route, send_sem, recv_sem, step, 2)
+
+    def wait_all(copies):
+        for copy in copies:
+            copy.wait_recv()
+
+    def rows_of(body, first, last, carry):
+        return lax.fori_loop(first, last, body, carry, unroll=3 if (last - first) % 3 == 0 else 4)
 
     def unpacked(pack_in, step):
         from_south = jnp.where(my > 0, roll_lanes(pack_in[step, 0], 1), zero)
@@ -165,16 +183,16 @@
     def row_of(ref, x):
         return jnp.broadcast_to(ref[pl.ds(x, 1), :], (SUB, LANE))
 
+    hslot = channels
+
     def send_state(step, packed, h):
-        packs[step] = packed_with(packed, h, channels)
         state[step, 1, hrow:hrow + SUB, :] = jnp.broadcast_to(h[0:1, :], (SUB, LANE))
         state[step, SUB, hrow:hrow + SUB, :] = jnp.broadcast_to(h[SUB - 1:SUB, :], (SUB, LANE))
-        return exchange(
-            state.at[step, SUB], state.at[step, 0], state.at[step, 1], state.at[step, SUB + 1],
-            packs.at[step], packr, f_send, f_recv, step,
+        row_copies = exchange_rows(
+            state.at[step, SUB], state.at[step, 0], state.at[step, 1], state.at[step, SUB + 1], f_send, f_recv, step,
         )
-
-    hslot = channels
+        packs[step] = packed_with(packed, h, hslot)
+        return row_copies, exchange_columns(packs.at[step], packr, f_send, f_recv, step)
 
     def pack_body(x, packed):
         for t in range(tiles):
@@ -182,20 +200,18 @@
         return packed
 
     heights = [height_ref[...]]
-    copies = send_state(0, lax.fori_loop(0, SUB, pack_body, zero), heights[0])
+    row_copies, column_copies = send_state(0, rows_of(pack_body, 0, SUB, zero), heights[0])
 
     for step in range(ITERS):
         h = heights[step]
         final = step == ITERS - 1
         damp = jnp.tanh(h)
-        for copy in copies:
-            copy.wait_recv()
+        wait_all(column_copies)
         columns = unpacked(packr, step)
         side = spread(columns, hslot)
-        h_w = jnp.where(first_row, jnp.broadcast_to(state[step, 0, hrow:hrow + 1, :], (SUB, LANE)), roll_rows(h, 1))
-        h_e = jnp.where(last_row, jnp.broadcast_to(state[step, SUB + 1, hrow:hrow + 1, :], (SUB, LANE)), roll_rows(h, SUB - 1))
         h_s = jnp.where(first_lane, side, roll_lanes(h, 1))
         h_n = jnp.where(last_lane, side, roll_lanes(h, LANE - 1))
+        h_w, h_e = roll_rows(h, 1), roll_rows(h, SUB - 1)
         arow[step, 1:SUB + 1, :] = (-0.25 * ADVECTION) * (h_n - h_s)
         brow[step] = (0.25 * ADVECTION) * (h_e - h_w)
 
@@ -227,16 +243,37 @@
                     packed = packed_with(packed, new, x * tiles + t)
             return packed
 
-        packed = lax.fori_loop(0, SUB, forward_body, zero)
-        if not final:
-            lap = h_e + h_w + h_n + h_s - 4.0 * h
-            h = h + HEIGHT_DIFFUSION * lap - HEIGHT_DAMPING * damp + (BUOYANCY / levels) * wet_tile * mrow[...]
-            heights.append(h)
-            copies = send_state(step + 1, packed, h)
+        if final:
+            rows_of(forward_body, 0, SUB, zero)
+            break
+        packed = rows_of(forward_body, 1, SUB - 1, zero)
+        wait_all(row_copies)
+        h_w = jnp.where(first_row, jnp.broadcast_to(state[step, 0, hrow:hrow + 1, :], (SUB, LANE)), h_w)
+        h_e = jnp.where(last_row, jnp.broadcast_to(state[step, SUB + 1, hrow:hrow + 1, :], (SUB, LANE)), h_e)
+        brow[step] = (0.25 * ADVECTION) * (h_e - h_w)
+        packed = forward_body(SUB - 1, forward_body(0, packed))
+        lap = h_e + h_w + h_n + h_s - 4.0 * h
+        h = h + HEIGHT_DIFFUSION * lap - HEIGHT_DAMPING * damp + (BUOYANCY / levels) * wet_tile * mrow[...]
+        heights.append(h)
+        row_copies, column_copies = send_state(step + 1, packed, h)
+
+    def add_rows(step):
+        for t in range(tiles):
+            rows = slice(t * SUB, (t + 1) * SUB)
+            lam[0, rows, :] = lam[0, rows, :] + slab_r[step, 0, rows, :]
+            lam[SUB - 1, rows, :] = lam[SUB - 1, rows, :] + slab_r[step, 1, rows, :]
+
+    def height_arrivals(step, lam_h, columns):
+        lam_h = lam_h + jnp.where(edge_lane, spread(columns, hslot), 0.0)
+        lam_h = lam_h + jnp.where(first_row, jnp.broadcast_to(slab_r[step, 0, hrow:hrow + 1, :], (SUB, LANE)), 0.0)
+        return lam_h + jnp.where(last_row, jnp.broadcast_to(slab_r[step, 1, hrow:hrow + 1, :], (SUB, LANE)), 0.0)
 
     lam_h = hw_ref[...]
     columns = None
     for step in reversed(range(ITERS)):
+        if step < ITERS - 1:
+            wait_all(column_copies)
+            columns = unpacked(bpackr, step + 1)
 
         def gather_body(x, packed):
             b = row_of(brow.at[step], x)
@@ -260,12 +297,20 @@
             gvrow[pl.ds(x, 1), :] = jnp.sum(gv, axis=0, keepdims=True)
             return packed
 
-        packed = lax.fori_loop(0, SUB, gather_body, zero)
+        packed = rows_of(gather_body, 1, SUB - 1, zero)
+        wait_all(row_copies)
+        if step == ITERS - 1:
+            h_w = jnp.where(first_row, jnp.broadcast_to(state[step, 0, hrow:hrow + 1, :], (SUB, LANE)), h_w)
+            h_e = jnp.where(last_row, jnp.broadcast_to(state[step, SUB + 1, hrow:hrow + 1, :], (SUB, LANE)), h_e)
+            brow[step] = (0.25 * ADVECTION) * (h_e - h_w)
+        else:
+            add_rows(step + 1)
+            lam_h = height_arrivals(step + 1, lam_h, columns)
+        packed = gather_body(SUB - 1, gather_body(0, packed))
         gu = (-0.25 * ADVECTION) * gurow[...]
         gv = (-0.25 * ADVECTION) * gvrow[...]
         spread_h = HEIGHT_DIFFUSION * lam_h
         to_e, to_w, to_n, to_s = spread_h + gv, spread_h - gv, spread_h - gu, spread_h + gu
-        bpacks[step] = packed_with(packed, jnp.where(last_lane, to_n, to_s), hslot)
         a_last = row_of(arow.at[step], SUB)
         a_first = row_of(arow.at[step], 1)
         for t in range(tiles):
@@ -274,13 +319,13 @@
             slab_s[step, 1, rows, :] = (diff[t] + a_first) * mu[1, rows, :]
         slab_s[step, 0, hrow:hrow + SUB, :] = jnp.broadcast_to(to_e[SUB - 1:SUB, :], (SUB, LANE))
         slab_s[step, 1, hrow:hrow + SUB, :] = jnp.broadcast_to(to_w[0:1, :], (SUB, LANE))
-        copies = exchange(
-            slab_s.at[step, 0], slab_r.at[step, 0], slab_s.at[step, 1], slab_r.at[step, 1],
-            bpacks.at[step], bpackr, b_send, b_recv, step,
+        row_copies = exchange_rows(
+            slab_s.at[step, 0], slab_r.at[step, 0], slab_s.at[step, 1], slab_r.at[step, 1], b_send, b_recv, step,
         )
-
-        source = (BUOYANCY / levels) * wet_tile * lam_h
-        mrow[...] = source
+        bpacks[step] = packed_with(packed, jnp.where(last_lane, to_n, to_s), hslot)
+        column_copies = exchange_columns(bpacks.at[step], bpackr, b_send, b_recv, step)
+
+        mrow[...] = (BUOYANCY / levels) * wet_tile * lam_h
 
         def local_body(x, carry):
             a_w = row_of(arow.at[step], x)
@@ -305,29 +350,29 @@
                 lam[x, rows, :] = value
             return carry
 
-        lax.fori_loop(0, SUB, local_body, 0)
+        rows_of(local_body, 0, SUB, 0)
         damp = jnp.tanh(heights[step])
         lam_h = (
             lam_h - 4.0 * spread_h - HEIGHT_DAMPING * (1.0 - damp * damp) * lam_h
             + jnp.where(first_row, 0.0, roll_rows(to_e, 1)) + jnp.where(last_row, 0.0, roll_rows(to_w, SUB - 1))
             + jnp.where(first_lane, 0.0, roll_lanes(to_n, 1)) + jnp.where(last_lane, 0.0, roll_lanes(to_s, LANE - 1))
         )
-        for copy in copies:
-            copy.wait_recv()
-        columns = unpacked(bpackr, step)
-        for t in range(tiles):
-            rows = slice(t * SUB, (t + 1) * SUB)
-            lam[0, rows, :] = lam[0, rows, :] + slab_r[step, 0, rows, :]
-            lam[SUB - 1, rows, :] = lam[SUB - 1, rows, :] + slab_r[step, 1, rows, :]
-        lam_h = lam_h + jnp.where(edge_lane, spread(columns, hslot), 0.0)
-        lam_h = lam_h + jnp.where(first_row, jnp.broadcast_to(slab_r[step, 0, hrow:hrow + 1, :], (SUB, LANE)), 0.0)
-        lam_h = lam_h + jnp.where(last_row, jnp.broadcast_to(slab_r[step, 1, hrow:hrow + 1, :], (SUB, LANE)), 0.0)
-
-    outh_ref[...] = lam_h
-    for x in range(SUB):
+
+    wait_all(column_copies)
+    columns = unpacked(bpackr, 0)
+
+    def write_row(x):
         for t in range(tiles):
             value = lam[x, t * SUB:(t + 1) * SUB, :] + jnp.where(edge_lane, spread(columns, x * tiles + t), 0.0)
             out_ref[pl.ds(t * SUB * SUB + x, SUB, stride=SUB), :] = value
+
+    for x in range(1, SUB - 1):
+        write_row(x)
+    wait_all(row_copies)
+    add_rows(0)
+    write_row(0)
+    write_row(SUB - 1)
+    outh_ref[...] = height_arrivals(0, lam_h, columns)
 
     for copy in a2a + sends:
         copy.wait_send()
@@ -344,7 +389,6 @@
     rows = channels + SUB
     f32 = jnp.float32
     vmem = pl.BlockSpec(memory_space=pltpu.VMEM)
-    smem = pl.BlockSpec(memory_space=pltpu.SMEM)
     tile = pltpu.VMEM((SUB, LANE), f32)
     out, out_h = pl.pallas_call(
         functools.partial(kernel, n, n_y, levels, piece_rows),
@@ -352,7 +396,7 @@
             jax.ShapeDtypeStruct((channels * SUB, LANE), f32),
             jax.ShapeDtypeStruct((SUB, LANE), f32),
         ),
-        in_specs=[smem, smem, vmem, vmem, vmem, pl.BlockSpec(memory_space=pl.ANY), vmem],
+        in_specs=[pl.BlockSpec(memory_space=pltpu.HBM)] * 7,
         out_specs=(vmem, vmem),
         scratch_shapes=[
             pltpu.VMEM((n * padded, LANE), f32),
@@ -372,13 +416,19 @@
             pltpu.VMEM((ITERS, 2, rows, LANE), f32),
             pltpu.VMEM((ITERS, SUB, LANE), f32),
             pltpu.VMEM((ITERS, 2, SUB, LANE), f32),
+            pltpu.SMEM(holder_list.shape, jnp.int32),
+            pltpu.SMEM(diffusivity.shape, f32),
+            pltpu.VMEM(checkpoint.shape[2:], f32),
+            tile,
+            pltpu.VMEM((SUB, LANE), jnp.int32),
+            tile,
             pltpu.SemaphoreType.DMA((n,)),
             pltpu.SemaphoreType.DMA((n,)),
             pltpu.SemaphoreType.DMA((ITERS, 4)),
             pltpu.SemaphoreType.DMA((ITERS, 4)),
             pltpu.SemaphoreType.DMA((ITERS, 4)),
             pltpu.SemaphoreType.DMA((ITERS, 4)),
-            pltpu.SemaphoreType.DMA,
+            pltpu.SemaphoreType.DMA((7,)),
         ],
         compiler_params=pltpu.CompilerParams(
             collective_id=0, has_side_effects=True, vmem_limit_bytes=32 * 2**20

time: 60.8 us -> 51.1 us (0.84)
  Pallas kernels: 54 us -> 44.3 us
    pallas_call x1, Pallas kernels: 54 us -> 44.3 us  [local(): pl.pallas_call(functools.partial(kernel, n, n_y, levels, piece_rows), out...]
where the time goes in v2:
time: 51.1 us; the launch traced here: 50.8 us
  Pallas kernels  44.3 us (87%)
  local copies, waits for them, and re-layouts  5.85 us (11%)
  between operations  0.66 us (1%)
    pallas_call x1, Pallas kernels, local(): pl.pallas_call(functools.partial(kernel, n, n_y, levels, piece_rows), out...  44.3 us
    unnamed x16, local copies, waits for them, and re-layouts  5.85 us

profile of v2, /device:TPU:0, one launch (start us, length us, event | category | flops | bytes accessed | tf_op | source)
XLA Modules:
  0.0 50.8 jit_solution(9048365210040715438)
XLA Ops:
  0.6 0.0 copy-start.5
  0.6 0.0 copy-start.6
  0.7 0.7 %copy-done.5 = f32[3,16]{1,0:T(4,128)S(1)} copy-done((f32[3,16]{1,0:T(4,128)S(1)}, f32[3,16]{1,0:T(4,128)}, u32[]{:S(2)}) %copy-start.5) | copy-done | bytes 216
  1.3 0.0 copy-done.6
  1.3 0.0 copy-start
  1.3 0.9 %copy-done = f32[1,1,4,12288]{3,2,1,0:T(4,128)S(1)} copy-done((f32[1,1,4,12288]{3,2,1,0:T(4,128)S(1)}, f32[1,1,4,12288]{3,2,1,0:T(4,128)}, u32[]{:S(2)}) %copy-start) | copy-done | bytes 196632
  2.2 0.0 copy-start.1
  2.2 0.9 %copy-done.1 = f32[3,16,8,128]{3,2,1,0:T(8,128)S(1)} copy-done((f32[3,16,8,128]{3,2,1,0:T(8,128)S(1)}, f32[3,16,8,128]{3,2,1,0:T(8,128)}, u32[]{:S(2)}) %copy-start.1) | copy-done | bytes 196632
  3.2 0.0 copy-start.2
  3.2 0.7 %copy-done.2 = f32[8,128]{1,0:T(8,128)S(1)} copy-done((f32[8,128]{1,0:T(8,128)S(1)}, f32[8,128]{1,0:T(8,128)}, u32[]{:S(2)}) %copy-start.2) | copy-done | bytes 4120
  3.9 0.0 copy-start.3
  3.9 0.7 %copy-done.3 = s32[8,128]{1,0:T(8,128)S(1)} copy-done((s32[8,128]{1,0:T(8,128)S(1)}, s32[8,128]{1,0:T(8,128)}, u32[]{:S(2)}) %copy-start.3) | copy-done | bytes 4120
  4.5 0.0 copy-start.4
  4.5 0.7 %copy-done.4 = f32[8,128]{1,0:T(8,128)S(1)} copy-done((f32[8,128]{1,0:T(8,128)S(1)}, f32[8,128]{1,0:T(8,128)}, u32[]{:S(2)}) %copy-start.4) | copy-done | bytes 4120
  5.2 44.3 %shard_map.86 = (f32[384,128]{1,0:T(8,128)S(1)}, f32[8,128]{1,0:T(8,128)S(1)}) custom-call(s32[1,1,4]{2,1,0:T(1,128)S(1)} %copy-done.6, f32[3,16]{1,0:T(4,128)S(1)} %copy-done.5, f32[4,12288]{1,0:T(4,128)S(1)} %bitcast.3, f32[8,128]{1,0:T(8,128)S(1)} %copy-done.2, s32[8,128]{1,0:T(8,128)S(1)} %copy-done.3, f32[384,128]{1,0:T(8,128)S(1)} %bitcast.4, ...), custom_call_target="tpu_custom_call" | custom-call | tf_op jit(solution)/shard_map/pallas_call | solution.py:393
  49.5 0.7 %copy.11 = f32[3,16,8,128]{3,2,1,0:T(8,128)} copy(f32[3,16,8,128]{3,2,1,0:T(8,128)S(1)} %bitcast.5) | data formatting | bytes 393216
  50.2 0.6 %copy.12 = f32[8,128]{1,0:T(8,128)} copy(f32[8,128]{1,0:T(8,128)S(1)} %get-tuple-element.9) | data formatting | bytes 8192
Async XLA Ops:
  0.6 0.7 %copy-start.5 = (f32[3,16]{1,0:T(4,128)S(1)}, f32[3,16]{1,0:T(4,128)}, u32[]{:S(2)}) copy-start(f32[3,16]{1,0:T(4,128)} %diff_hbm.1) | copy-start | bytes 580
  0.6 0.7 %copy-start.6 = (s32[1,1,4]{2,1,0:T(1,128)S(1)}, s32[1,1,4]{2,1,0:T(1,128)}, u32[]{:S(2)}) copy-start(s32[1,1,4]{2,1,0:T(1,128)} %holder_hbm.1) | copy-start | bytes 52
  1.3 0.9 %copy-start = (f32[1,1,4,12288]{3,2,1,0:T(4,128)S(1)}, f32[1,1,4,12288]{3,2,1,0:T(4,128)}, u32[]{:S(2)}) copy-start(f32[1,1,4,12288]{3,2,1,0:T(4,128)} %param.7) | copy-start | bytes 589828
  2.2 0.9 %copy-start.1 = (f32[3,16,8,128]{3,2,1,0:T(8,128)S(1)}, f32[3,16,8,128]{3,2,1,0:T(8,128)}, u32[]{:S(2)}) copy-start(f32[3,16,8,128]{3,2,1,0:T(8,128)} %param.12) | copy-start | bytes 589828
  3.2 0.7 %copy-start.2 = (f32[8,128]{1,0:T(8,128)S(1)}, f32[8,128]{1,0:T(8,128)}, u32[]{:S(2)}) copy-start(f32[8,128]{1,0:T(8,128)} %height_hbm.1) | copy-start | bytes 12292
  3.9 0.7 %copy-start.3 = (s32[8,128]{1,0:T(8,128)S(1)}, s32[8,128]{1,0:T(8,128)}, u32[]{:S(2)}) copy-start(s32[8,128]{1,0:T(8,128)} %mask_hbm.1) | copy-start | bytes 12292
  4.5 0.7 %copy-start.4 = (f32[8,128]{1,0:T(8,128)S(1)}, f32[8,128]{1,0:T(8,128)}, u32[]{:S(2)}) copy-start(f32[8,128]{1,0:T(8,128)} %hw_hbm.1) | copy-start | bytes 12292

commit v3 on v2

--- a/solution.py
+++ b/solution.py
@@ -31,7 +31,7 @@
     holder_hbm, diff_hbm, ckpt_hbm, height_hbm, mask_hbm, tw_hbm, hw_hbm,
     out_ref, outh_ref,
     buf, recv, state, dy, tw, lam, mu, wet, arow, brow, mrow, gurow, gvrow,
-    packs, packr, slab_s, slab_r, bpacks, bpackr,
+    packs, packr, dpacks, dpackr, slab_s, slab_r, bpacks, bpackr,
     holder_ref, diff_ref, ckpt_ref, height_ref, mask_ref, hw_ref,
     a2a_send, a2a_recv, f_send, f_recv, b_send, b_recv, in_sem,
 ):
@@ -58,6 +58,8 @@
         pl.semaphore_signal(barrier, inc=1, device_id={"gx": lax.rem(me + k, n)}, device_id_type=MESH)
     for other in (north, south):
         pl.semaphore_signal(barrier, inc=1, device_id={"gy": other}, device_id_type=MESH)
+        for side in (east, west):
+            pl.semaphore_signal(barrier, inc=1, device_id={"gx": side, "gy": other}, device_id_type=MESH)
 
     loads[0].wait()
     depth = 0 if piece_rows % SUB else piece_rows // SUB
@@ -69,7 +71,7 @@
             row = r % SUB * depth + r // SUB if depth else r
             buf[pl.ds(o * padded + row, size, stride=padded), :] = ckpt_ref[o:o + size, r * LANE:(r + 1) * LANE]
 
-    pl.semaphore_wait(barrier, n + 1)
+    pl.semaphore_wait(barrier, n + 5)
 
     mine = pl.multiple_of(me * padded, SUB)
     sends = []
@@ -97,7 +99,8 @@
 
     for load in loads[1:]:
         load.wait()
-    mrow[...] = zero
+    mrow[0:SUB, :] = zero
+    mrow[SUB:2 * SUB, :] = zero
     diff = []
     for t in range(tiles):
         value = zero
@@ -106,7 +109,7 @@
             value = jnp.where(sub == s, diff_ref[channel // levels, channel % levels], value)
         diff.append(value)
     wet_tile = mask_ref[...].astype(jnp.float32)
-    wet[...] = wet_tile
+    wet[1:SUB + 1, :] = wet_tile
     for t in range(tiles):
         rows = pl.ds(t * SUB, SUB)
         mu[0, rows, :] = zero
@@ -124,11 +127,11 @@
         holder = holder_ref[0, 0, p]
         if depth:
             for x in range(SUB):
-                state[0, x + 1, p * depth:(p + 1) * depth, :] = recv[holder, x * depth:(x + 1) * depth, :]
+                state[0, x + 2, p * depth:(p + 1) * depth, :] = recv[holder, x * depth:(x + 1) * depth, :]
         else:
             for r in range(piece_rows):
                 row = p * piece_rows + r
-                state[0, row % SUB + 1, row // SUB:row // SUB + 1, :] = recv[holder, r:r + 1, :]
+                state[0, row % SUB + 2, row // SUB:row // SUB + 1, :] = recv[holder, r:r + 1, :]
 
     def exchange(route, send_sem, recv_sem, step, first):
         copies = []
@@ -157,9 +160,9 @@
     def rows_of(body, first, last, carry):
         return lax.fori_loop(first, last, body, carry, unroll=3 if (last - first) % 3 == 0 else 4)
 
-    def unpacked(pack_in, step):
-        from_south = jnp.where(my > 0, roll_lanes(pack_in[step, 0], 1), zero)
-        from_north = jnp.where(my < n_y - 1, roll_lanes(pack_in[step, 1], LANE - 1), zero)
+    def unpacked(south_value, north_value, distance=1):
+        from_south = jnp.where(my > 0, roll_lanes(south_value, distance), zero)
+        from_north = jnp.where(my < n_y - 1, roll_lanes(north_value, LANE - distance), zero)
         return jnp.where(even, from_north, from_south)
 
     def spread(columns, k):
@@ -184,78 +187,222 @@
         return jnp.broadcast_to(ref[pl.ds(x, 1), :], (SUB, LANE))
 
     hslot = channels
-
-    def send_state(step, packed, h):
-        state[step, 1, hrow:hrow + SUB, :] = jnp.broadcast_to(h[0:1, :], (SUB, LANE))
-        state[step, SUB, hrow:hrow + SUB, :] = jnp.broadcast_to(h[SUB - 1:SUB, :], (SUB, LANE))
-        row_copies = exchange_rows(
-            state.at[step, SUB], state.at[step, 0], state.at[step, 1], state.at[step, SUB + 1], f_send, f_recv, step,
+    width = 2 * tiles
+    span = width * SUB
+    lead = pair == 0
+    for x in range(1, SUB):
+        lead = lead | (pair == x * tiles)
+    strip_diff = zero
+    for t in range(tiles):
+        strip_diff = strip_diff + diff[t] * roll_lanes(jnp.where(lead, 1.0, 0.0), 2 * t)
+    inside = (jnp.where(even, n_y - 1 - my, my) > 0) & (lane < span)
+    top_tile = (pair & (per - 1)) == 0
+    low_tile = (pair & (per - 1)) == per - 1
+
+    def whole_row(value, x):
+        return jnp.broadcast_to(value[x:x + 1, :], (SUB, LANE))
+
+    def repeated(value):
+        value = value + roll_lanes(value, 2)
+        return value + roll_lanes(value, 4) + roll_lanes(value, 8)
+
+    def row_strips(value):
+        near, far = zero, zero
+        for x in range(SUB):
+            k = x * tiles
+            moved = roll_lanes(whole_row(value, x), 2 * k + 1)
+            near = jnp.where(pair == k, moved, near)
+            far = jnp.where((lane == (2 * k + LANE - 1) % LANE) | (lane == 2 * k + 2), moved, far)
+        return repeated(near), repeated(far)
+
+    def send_rows(step, h):
+        for x in (0, 1, SUB - 2, SUB - 1):
+            state[step, x + 2, hrow:hrow + SUB, :] = jnp.where(sub < SUB // 2, whole_row(h, x), whole_row(wet_tile, x))
+        return exchange_rows(
+            state.at[step, pl.ds(SUB, 2)], state.at[step, pl.ds(0, 2)],
+            state.at[step, pl.ds(2, 2)], state.at[step, pl.ds(SUB + 2, 2)], f_send, f_recv, step,
         )
-        packs[step] = packed_with(packed, h, hslot)
-        return row_copies, exchange_columns(packs.at[step], packr, f_send, f_recv, step)
+
+    def send_corners(step, packed, h):
+        dpacks[step, 0] = packed_with(packed, h, hslot)
+        dpacks[step, 1] = row_strips(h)[0]
+        route = []
+        for i, (x_to, y_to) in enumerate(((east, north), (east, south), (west, north), (west, south))):
+            route.append((dpacks.at[step], dpackr.at[step, i], {"gx": x_to, "gy": y_to}))
+        return exchange(route, f_send, f_recv, step, 4)
+
+    def send_columns(step, packed, far, h):
+        packs[step, 0] = packed_with(packed, h, hslot)
+        packs[step, 1] = far
+        packs[step, 2], packs[step, 3] = row_strips(h)
+        packs[step, 4] = wet_near
+        return exchange_columns(packs.at[step], packr, f_send, f_recv, step)
+
+    def pack_row(value, k, packed):
+        near, far = packed
+        moved = roll_lanes(value, 2 * k + 1)
+        before, after = lax.rem(2 * k + LANE - 1, LANE), 2 * k + 2
+        return jnp.where(pair == k, moved, near), jnp.where((lane == before) | (lane == after), moved, far)
 
     def pack_body(x, packed):
         for t in range(tiles):
-            packed = packed_with(packed, state[0, x + 1, t * SUB:(t + 1) * SUB, :], x * tiles + t)
+            packed = pack_row(state[0, x + 2, t * SUB:(t + 1) * SUB, :], x * tiles + t, packed)
         return packed
 
+    wet_near = row_strips(wet_tile)[0]
     heights = [height_ref[...]]
-    row_copies, column_copies = send_state(0, rows_of(pack_body, 0, SUB, zero), heights[0])
-
-    for step in range(ITERS):
+    row_copies = send_rows(0, heights[0])
+    packed = pack_body(SUB - 1, pack_body(0, (zero, zero)))
+    corner_copies = send_corners(0, packed[0], heights[0])
+    packed = rows_of(pack_body, 1, SUB - 1, packed)
+    column_copies = send_columns(0, packed[0], packed[1], heights[0])
+    strip_wet = None
+
+    def forward_row(step, x, k, columns, packed, update, own):
+        a = row_of(arow.at[step], x + 1)
+        b = row_of(brow.at[step], x + 1)
+        w = row_of(wet, x + 1)
+        centre = [state[step, x + 2, t * SUB:(t + 1) * SUB, :] for t in range(tiles)]
+        if update:
+            vert = vertical(centre)
+            total = centre[0]
+            for i in range(1, per):
+                total = total + centre[i]
+            mrow[pl.ds(x + 1, 1), :] = jnp.sum(total, axis=0, keepdims=True)
+        for t in range(tiles):
+            rows = slice(t * SUB, (t + 1) * SUB)
+            c = centre[t]
+            side = spread(columns, k + t)
+            c_s = jnp.where(first_lane, side, roll_lanes(c, 1))
+            c_n = jnp.where(last_lane, side, roll_lanes(c, LANE - 1))
+            delta = c_n - c_s
+            if own:
+                dy[step, x, rows, :] = delta
+            if update:
+                c_e = state[step, x + 3, rows, :]
+                c_w = state[step, x + 1, rows, :]
+                lap = c_e + c_w + c_n + c_s - 4.0 * c
+                new = c + w * (diff[t] * lap - a * (c_e - c_w) - b * delta + VERTICAL_MIX * vert[t])
+                state[step + 1, x + 2, rows, :] = new
+                if packed is not None:
+                    packed = pack_row(new, k + t, packed)
+        return packed
+
+    def next_height(h, h_e, h_w, h_n, h_s, w, total):
+        lap = h_e + h_w + h_n + h_s - 4.0 * h
+        return h + HEIGHT_DIFFUSION * lap - HEIGHT_DAMPING * jnp.tanh(h) + (BUOYANCY / levels) * w * total
+
+    def along_latitude(h, side):
+        h_n = jnp.where(last_lane, side, roll_lanes(h, LANE - 1))
+        h_s = jnp.where(first_lane, side, roll_lanes(h, 1))
+        return h_n, h_s
+
+    for step in range(0, ITERS, 2):
         h = heights[step]
-        final = step == ITERS - 1
-        damp = jnp.tanh(h)
         wait_all(column_copies)
-        columns = unpacked(packr, step)
-        side = spread(columns, hslot)
-        h_s = jnp.where(first_lane, side, roll_lanes(h, 1))
-        h_n = jnp.where(last_lane, side, roll_lanes(h, LANE - 1))
+        received = [
+            unpacked(packr[step, 0, slot], packr[step, 1, slot], distance)
+            for slot, distance in ((0, 1), (1, 2), (2, 1), (3, 2), (4, 1))
+        ]
+        columns, far_columns, strip_h, far_h, strip_w = received
+        strip_wet = strip_w if step == 0 else strip_wet
+        h_n, h_s = along_latitude(h, spread(columns, hslot))
         h_w, h_e = roll_rows(h, 1), roll_rows(h, SUB - 1)
         arow[step, 1:SUB + 1, :] = (-0.25 * ADVECTION) * (h_n - h_s)
-        brow[step] = (0.25 * ADVECTION) * (h_e - h_w)
-
-        def forward_body(x, packed):
-            a = row_of(arow.at[step], x + 1)
-            b = row_of(brow.at[step], x)
-            w = row_of(wet, x)
-            centre = [state[step, x + 1, t * SUB:(t + 1) * SUB, :] for t in range(tiles)]
-            if not final:
-                vert = vertical(centre)
-                total = centre[0]
-                for i in range(1, per):
-                    total = total + centre[i]
-                mrow[pl.ds(x, 1), :] = jnp.sum(total, axis=0, keepdims=True)
-            for t in range(tiles):
-                rows = slice(t * SUB, (t + 1) * SUB)
-                c = centre[t]
-                side = spread(columns, x * tiles + t)
-                c_s = jnp.where(first_lane, side, roll_lanes(c, 1))
-                c_n = jnp.where(last_lane, side, roll_lanes(c, LANE - 1))
-                delta = c_n - c_s
-                dy[step, x, rows, :] = delta
-                if not final:
-                    c_e = state[step, x + 2, rows, :]
-                    c_w = state[step, x, rows, :]
-                    lap = c_e + c_w + c_n + c_s - 4.0 * c
-                    new = c + w * (diff[t] * lap - a * (c_e - c_w) - b * delta + VERTICAL_MIX * vert[t])
-                    state[step + 1, x + 1, rows, :] = new
-                    packed = packed_with(packed, new, x * tiles + t)
-            return packed
+        brow[step, 1:SUB + 1, :] = (0.25 * ADVECTION) * (h_e - h_w)
+
+        def inner_body(x, carry):
+            forward_row(step, x, x * tiles, columns, None, True, True)
+            return carry
+
+        rows_of(inner_body, 1, SUB - 1, 0)
+        wait_all(row_copies)
+        wait_all(corner_copies)
+        corner_w, corner_e = (unpacked(dpackr[step, i, 0], dpackr[step, i + 1, 0]) for i in (0, 2))
+        corner_hw, corner_he = (unpacked(dpackr[step, i, 1], dpackr[step, i + 1, 1]) for i in (0, 2))
+        ring = []
+        for x, far_x, near, corner, row in (
+            (-1, 0, 0, corner_w, SUB - 1), (SUB, SUB + 3, SUB - 1, corner_e, 0),
+        ):
+            h_ring = jnp.broadcast_to(state[step, x + 2, hrow:hrow + 1, :], (SUB, LANE))
+            h_out = jnp.broadcast_to(state[step, far_x, hrow:hrow + 1, :], (SUB, LANE))
+            h_in = whole_row(h, near)
+            if step == 0:
+                wet[x + 1:x + 2, :] = state[step, x + 2, hrow + SUB // 2:hrow + SUB // 2 + 1, :]
+            ring_n, ring_s = along_latitude(h_ring, whole_row(spread(corner, hslot), row))
+            ring_e, ring_w = (h_in, h_out) if x < 0 else (h_out, h_in)
+            arow[step, x + 1:x + 2, :] = ((-0.25 * ADVECTION) * (ring_n - ring_s))[0:1, :]
+            brow[step, x + 1:x + 2, :] = ((0.25 * ADVECTION) * (ring_e - ring_w))[0:1, :]
+            forward_row(step, x, row * tiles, corner, None, True, False)
+            ring.append((
+                h_ring, next_height(h_ring, ring_e, ring_w, ring_n, ring_s, row_of(wet, x + 1), row_of(mrow, x + 1)),
+            ))
+        h_w = jnp.where(first_row, ring[0][0], h_w)
+        h_e = jnp.where(last_row, ring[1][0], h_e)
+        brow[step, 1:SUB + 1, :] = (0.25 * ADVECTION) * (h_e - h_w)
+        for x in (0, SUB - 1):
+            forward_row(step, x, x * tiles, columns, None, True, True)
+        h_next = next_height(h, h_e, h_w, h_n, h_s, wet_tile, mrow[1:SUB + 1, :])
+
+        def strip_sides(value, from_e, from_w):
+            e = jnp.where(lane >= span - width, roll_lanes(from_e, span - width), roll_lanes(value, LANE - width))
+            w = jnp.where(lane < width, roll_lanes(from_w, LANE - span + width), roll_lanes(value, width))
+            return e, w
+
+        own = packs[step, 0]
+        own_h = packs[step, 2]
+        c_e, c_w = strip_sides(columns, corner_e, corner_w)
+        c_n, c_s = jnp.where(even, far_columns, own), jnp.where(even, own, far_columns)
+        s_e, s_w = strip_sides(strip_h, corner_he, corner_hw)
+        s_n, s_s = jnp.where(even, far_h, own_h), jnp.where(even, own_h, far_h)
+        down, up = roll_rows(columns, 1), roll_rows(columns, SUB - 1)
+        upper = jnp.where(first_row, jnp.where(top_tile, columns, roll_lanes(down, 2)), down)
+        lower = jnp.where(last_row, jnp.where(low_tile, columns, roll_lanes(up, LANE - 2)), up)
+        a = (-0.25 * ADVECTION) * (s_n - s_s)
+        b = (0.25 * ADVECTION) * (s_e - s_w)
+        lap = c_e + c_w + c_n + c_s - 4.0 * columns
+        strip = columns + strip_wet * (
+            strip_diff * lap - a * (c_e - c_w) - b * (c_n - c_s) + VERTICAL_MIX * (upper + lower - 2.0 * columns)
+        )
+        sums = jnp.broadcast_to(jnp.sum(columns, axis=0, keepdims=True), (SUB, LANE))
+        total = sums
+        for i in range(1, per):
+            total = total + roll_lanes(sums, LANE - 2 * i)
+        total = repeated(jnp.where(lead, total, 0.0))
+        strip_h = next_height(strip_h, s_e, s_w, s_n, s_s, strip_wet, total)
+        columns = jnp.where(inside, strip, 0.0)
+        strip_h = jnp.where(inside, strip_h, 0.0)
+        side = zero
+        for x in range(SUB):
+            side = jnp.where(sub == x, spread(strip_h, x * tiles), side)
+
+        step += 1
+        final = step == ITERS - 1
+        h = h_next
+        heights.append(h)
+        h_n, h_s = along_latitude(h, side)
+        h_w = jnp.where(first_row, ring[0][1], roll_rows(h, 1))
+        h_e = jnp.where(last_row, ring[1][1], roll_rows(h, SUB - 1))
+        arow[step, 1:SUB + 1, :] = (-0.25 * ADVECTION) * (h_n - h_s)
+        brow[step, 1:SUB + 1, :] = (0.25 * ADVECTION) * (h_e - h_w)
+
+        def second_body(x, packed):
+            done = forward_row(step, x, x * tiles, columns, None if final else packed, not final, True)
+            return packed if final else done
 
         if final:
-            rows_of(forward_body, 0, SUB, zero)
+            rows_of(second_body, 0, SUB, 0)
             break
-        packed = rows_of(forward_body, 1, SUB - 1, zero)
-        wait_all(row_copies)
-        h_w = jnp.where(first_row, jnp.broadcast_to(state[step, 0, hrow:hrow + 1, :], (SUB, LANE)), h_w)
-        h_e = jnp.where(last_row, jnp.broadcast_to(state[step, SUB + 1, hrow:hrow + 1, :], (SUB, LANE)), h_e)
-        brow[step] = (0.25 * ADVECTION) * (h_e - h_w)
-        packed = forward_body(SUB - 1, forward_body(0, packed))
-        lap = h_e + h_w + h_n + h_s - 4.0 * h
-        h = h + HEIGHT_DIFFUSION * lap - HEIGHT_DAMPING * damp + (BUOYANCY / levels) * wet_tile * mrow[...]
+        packed = (zero, zero)
+        for x in (0, 1, SUB - 2, SUB - 1):
+            packed = second_body(x, packed)
+        h_edges = next_height(h, h_e, h_w, h_n, h_s, wet_tile, mrow[1:SUB + 1, :])
+        row_copies = send_rows(step + 1, h_edges)
+        corner_copies = send_corners(step + 1, packed[0], h_edges)
+        packed = rows_of(second_body, 2, SUB - 2, packed)
+        h = next_height(h, h_e, h_w, h_n, h_s, wet_tile, mrow[1:SUB + 1, :])
         heights.append(h)
-        row_copies, column_copies = send_state(step + 1, packed, h)
+        column_copies = send_columns(step + 1, packed[0], packed[1], h)
 
     def add_rows(step):
         for t in range(tiles):
@@ -273,11 +420,11 @@
     for step in reversed(range(ITERS)):
         if step < ITERS - 1:
             wait_all(column_copies)
-            columns = unpacked(bpackr, step + 1)
+            columns = unpacked(bpackr[step + 1, 0], bpackr[step + 1, 1])
 
         def gather_body(x, packed):
-            b = row_of(brow.at[step], x)
-            w = row_of(wet, x)
+            b = row_of(brow.at[step], x + 1)
+            w = row_of(wet, x + 1)
             gu = zero
             gv = zero
             for t in range(tiles):
@@ -291,19 +438,15 @@
                 bm = b * m
                 dm = diff[t] * m
                 packed = packed_with(packed, jnp.where(last_lane, dm - bm, dm + bm), x * tiles + t)
-                gu = gu + m * (state[step, x + 2, rows, :] - state[step, x, rows, :])
+                gu = gu + m * (state[step, x + 3, rows, :] - state[step, x + 1, rows, :])
                 gv = gv + m * dy[step, x, rows, :]
             gurow[pl.ds(x, 1), :] = jnp.sum(gu, axis=0, keepdims=True)
             gvrow[pl.ds(x, 1), :] = jnp.sum(gv, axis=0, keepdims=True)
             return packed
 
         packed = rows_of(gather_body, 1, SUB - 1, zero)
-        wait_all(row_copies)
-        if step == ITERS - 1:
-            h_w = jnp.where(first_row, jnp.broadcast_to(state[step, 0, hrow:hrow + 1, :], (SUB, LANE)), h_w)
-            h_e = jnp.where(last_row, jnp.broadcast_to(state[step, SUB + 1, hrow:hrow + 1, :], (SUB, LANE)), h_e)
-            brow[step] = (0.25 * ADVECTION) * (h_e - h_w)
-        else:
+        if step < ITERS - 1:
+            wait_all(row_copies)
             add_rows(step + 1)
             lam_h = height_arrivals(step + 1, lam_h, columns)
         packed = gather_body(SUB - 1, gather_body(0, packed))
@@ -325,12 +468,12 @@
         bpacks[step] = packed_with(packed, jnp.where(last_lane, to_n, to_s), hslot)
         column_copies = exchange_columns(bpacks.at[step], bpackr, b_send, b_recv, step)
 
-        mrow[...] = (BUOYANCY / levels) * wet_tile * lam_h
+        mrow[0:SUB, :] = (BUOYANCY / levels) * wet_tile * lam_h
 
         def local_body(x, carry):
             a_w = row_of(arow.at[step], x)
             a_e = row_of(arow.at[step], x + 2)
-            b = row_of(brow.at[step], x)
+            b = row_of(brow.at[step], x + 1)
             centre = [mu[x + 1, t * SUB:(t + 1) * SUB, :] for t in range(tiles)]
             vert = vertical(centre)
             push = row_of(mrow, x)
@@ -359,7 +502,7 @@
         )
 
     wait_all(column_copies)
-    columns = unpacked(bpackr, 0)
+    columns = unpacked(bpackr[0, 0], bpackr[0, 1])
 
     def write_row(x):
         for t in range(tiles):
@@ -401,17 +544,20 @@
         scratch_shapes=[
             pltpu.VMEM((n * padded, LANE), f32),
             pltpu.VMEM((n, padded, LANE), f32),
-            pltpu.VMEM((ITERS, SUB + 2, rows, LANE), f32),
+            pltpu.VMEM((ITERS, SUB + 4, rows, LANE), f32),
             pltpu.VMEM((ITERS, SUB, channels, LANE), f32),
             pltpu.VMEM((channels * SUB, LANE), f32),
             pltpu.VMEM((SUB, channels, LANE), f32),
             pltpu.VMEM((SUB + 2, channels, LANE), f32),
-            tile,
+            pltpu.VMEM((2 * SUB, LANE), f32),
             pltpu.VMEM((ITERS, 2 * SUB, LANE), f32),
-            pltpu.VMEM((ITERS, SUB, LANE), f32),
-            tile, tile, tile,
-            pltpu.VMEM((ITERS, SUB, LANE), f32),
+            pltpu.VMEM((ITERS, 2 * SUB, LANE), f32),
+            pltpu.VMEM((2 * SUB, LANE), f32),
+            tile, tile,
+            pltpu.VMEM((ITERS, 5, SUB, LANE), f32),
+            pltpu.VMEM((ITERS, 2, 5, SUB, LANE), f32),
             pltpu.VMEM((ITERS, 2, SUB, LANE), f32),
+            pltpu.VMEM((ITERS, 4, 2, SUB, LANE), f32),
             pltpu.VMEM((ITERS, 2, rows, LANE), f32),
             pltpu.VMEM((ITERS, 2, rows, LANE), f32),
             pltpu.VMEM((ITERS, SUB, LANE), f32),
@@ -424,14 +570,14 @@
             tile,
             pltpu.SemaphoreType.DMA((n,)),
             pltpu.SemaphoreType.DMA((n,)),
-            pltpu.SemaphoreType.DMA((ITERS, 4)),
-            pltpu.SemaphoreType.DMA((ITERS, 4)),
+            pltpu.SemaphoreType.DMA((ITERS, 8)),
+            pltpu.SemaphoreType.DMA((ITERS, 8)),
             pltpu.SemaphoreType.DMA((ITERS, 4)),
             pltpu.SemaphoreType.DMA((ITERS, 4)),
             pltpu.SemaphoreType.DMA((7,)),
         ],
         compiler_params=pltpu.CompilerParams(
-            collective_id=0, has_side_effects=True, vmem_limit_bytes=32 * 2**20
+            collective_id=0, has_side_effects=True, vmem_limit_bytes=60 * 2**20
         ),
     )(
         holder_list, diffusivity, checkpoint.reshape(checkpoint.shape[2:]), height, land_mask,

time: 51.1 us -> 45.3 us (0.89)
  local copies, waits for them, and re-layouts: 5.85 us -> 2.21 us
  Pallas kernels: 44.3 us -> 42.3 us
    unnamed x16 -> x4, local copies, waits for them, and re-layouts: 5.85 us -> 2.21 us
    pallas_call x1, Pallas kernels: 44.3 us -> 42.3 us  [local(): pl.pallas_call(functools.partial(kernel, n, n_y, levels, piece_rows), out...]
where the time goes in v3:
time: 45.3 us; the launch traced here: 45.2 us
  Pallas kernels  42.3 us (93%)
  local copies, waits for them, and re-layouts  2.21 us (5%)
  between operations  0.65 us (1%)
    pallas_call x1, Pallas kernels, local(): pl.pallas_call(functools.partial(kernel, n, n_y, levels, piece_rows), out...  42.3 us
    unnamed x4, local copies, waits for them, and re-layouts  2.21 us

profile of v3, /device:TPU:0, one launch (start us, length us, event | category | flops | bytes accessed | tf_op | source)
XLA Modules:
  0.0 45.2 jit_solution(9673234587542198319)
XLA Ops:
  0.6 42.3 %shard_map.86 = (f32[384,128]{1,0:T(8,128)}, f32[8,128]{1,0:T(8,128)}) custom-call(s32[1,1,4]{2,1,0:T(1,128)} %holder_hbm.1, f32[3,16]{1,0:T(4,128)} %diff_hbm.1, f32[4,12288]{1,0:T(4,128)} %bitcast.3, f32[8,128]{1,0:T(8,128)} %height_hbm.1, s32[8,128]{1,0:T(8,128)} %mask_hbm.1, f32[384,128]{1,0:T(8,128)} %bitcast.4, f32[8,128]{1,0:T(8,128)} %hw_hbm.1), custom_call_target="tpu_custom_call" | custom-call | tf_op jit(solution)/shard_map/pallas_call | solution.py:536
  43.0 0.0 copy-start
  43.0 1.6 %copy.11 = f32[3,16,8,128]{3,2,1,0:T(8,128)} copy(f32[3,16,8,128]{3,2,1,0:T(8,128)} %bitcast.5) | data formatting | bytes 393216
  44.6 0.0 copy-done
  44.6 0.6 %copy.12 = f32[8,128]{1,0:T(8,128)} copy(f32[8,128]{1,0:T(8,128)S(1)} %copy-done) | data formatting | bytes 8192
Async XLA Ops:
  43.0 1.6 %copy-start = (f32[8,128]{1,0:T(8,128)S(1)}, f32[8,128]{1,0:T(8,128)}, u32[]{:S(2)}) copy-start(f32[8,128]{1,0:T(8,128)} %get-tuple-element.9) | copy-start | bytes 12292

commit v4 on v3

--- a/solution.py
+++ b/solution.py
@@ -99,6 +99,8 @@
 
     for load in loads[1:]:
         load.wait()
+    gurow[...] = zero
+    gvrow[...] = zero
     mrow[0:SUB, :] = zero
     mrow[SUB:2 * SUB, :] = zero
     diff = []
@@ -386,12 +388,11 @@
         arow[step, 1:SUB + 1, :] = (-0.25 * ADVECTION) * (h_n - h_s)
         brow[step, 1:SUB + 1, :] = (0.25 * ADVECTION) * (h_e - h_w)
 
-        def second_body(x, packed):
+        def second_body(x, packed, step=step, columns=columns, final=final):
             done = forward_row(step, x, x * tiles, columns, None if final else packed, not final, True)
             return packed if final else done
 
         if final:
-            rows_of(second_body, 0, SUB, 0)
             break
         packed = (zero, zero)
         for x in (0, 1, SUB - 2, SUB - 1):
@@ -444,16 +445,26 @@
             gvrow[pl.ds(x, 1), :] = jnp.sum(gv, axis=0, keepdims=True)
             return packed
 
-        packed = rows_of(gather_body, 1, SUB - 1, zero)
-        if step < ITERS - 1:
+        def first_body(x, packed):
+            second_body(x, 0)
+            return gather_body(x, packed)
+
+        def sides():
+            gu = (-0.25 * ADVECTION) * gurow[...]
+            gv = (-0.25 * ADVECTION) * gvrow[...]
+            return spread_h + gv, spread_h - gv, spread_h - gu, spread_h + gu
+
+        start = step == ITERS - 1
+        if start:
+            packed = first_body(SUB - 1, first_body(0, zero))
+        else:
+            packed = rows_of(gather_body, 1, SUB - 1, zero)
             wait_all(row_copies)
             add_rows(step + 1)
             lam_h = height_arrivals(step + 1, lam_h, columns)
-        packed = gather_body(SUB - 1, gather_body(0, packed))
-        gu = (-0.25 * ADVECTION) * gurow[...]
-        gv = (-0.25 * ADVECTION) * gvrow[...]
+            packed = gather_body(SUB - 1, gather_body(0, packed))
         spread_h = HEIGHT_DIFFUSION * lam_h
-        to_e, to_w, to_n, to_s = spread_h + gv, spread_h - gv, spread_h - gu, spread_h + gu
+        to_e, to_w, to_n, to_s = sides()
         a_last = row_of(arow.at[step], SUB)
         a_first = row_of(arow.at[step], 1)
         for t in range(tiles):
@@ -465,6 +476,9 @@
         row_copies = exchange_rows(
             slab_s.at[step, 0], slab_r.at[step, 0], slab_s.at[step, 1], slab_r.at[step, 1], b_send, b_recv, step,
         )
+        if start:
+            packed = rows_of(first_body, 1, SUB - 1, packed)
+            to_e, to_w, to_n, to_s = sides()
         bpacks[step] = packed_with(packed, jnp.where(last_lane, to_n, to_s), hslot)
         column_copies = exchange_columns(bpacks.at[step], bpackr, b_send, b_recv, step)
 

time: 45.3 us -> 45.1 us (level)
  no operation moved by 1% of the time
where the time goes in v4:
time: 45.1 us; the launch traced here: 44.9 us
  Pallas kernels  42.1 us (93%)
  local copies, waits for them, and re-layouts  2.21 us (5%)
  between operations  0.65 us (1%)
    pallas_call x1, Pallas kernels, local(): pl.pallas_call(functools.partial(kernel, n, n_y, levels, piece_rows), out...  42.1 us
    unnamed x4, local copies, waits for them, and re-layouts  2.21 us

profile of v4, /device:TPU:0, one launch (start us, length us, event | category | flops | bytes accessed | tf_op | source)
XLA Modules:
  0.0 44.9 jit_solution(18316722230309238934)
XLA Ops:
  0.6 42.1 %shard_map.86 = (f32[384,128]{1,0:T(8,128)}, f32[8,128]{1,0:T(8,128)}) custom-call(s32[1,1,4]{2,1,0:T(1,128)} %holder_hbm.1, f32[3,16]{1,0:T(4,128)} %diff_hbm.1, f32[4,12288]{1,0:T(4,128)} %bitcast.3, f32[8,128]{1,0:T(8,128)} %height_hbm.1, s32[8,128]{1,0:T(8,128)} %mask_hbm.1, f32[384,128]{1,0:T(8,128)} %bitcast.4, f32[8,128]{1,0:T(8,128)} %hw_hbm.1), custom_call_target="tpu_custom_call" | custom-call | tf_op jit(solution)/shard_map/pallas_call | solution.py:550
  42.7 0.0 copy-start
  42.7 1.6 %copy.11 = f32[3,16,8,128]{3,2,1,0:T(8,128)} copy(f32[3,16,8,128]{3,2,1,0:T(8,128)} %bitcast.5) | data formatting | bytes 393216
  44.3 0.0 copy-done
  44.3 0.6 %copy.12 = f32[8,128]{1,0:T(8,128)} copy(f32[8,128]{1,0:T(8,128)S(1)} %copy-done) | data formatting | bytes 8192
Async XLA Ops:
  42.7 1.6 %copy-start = (f32[8,128]{1,0:T(8,128)S(1)}, f32[8,128]{1,0:T(8,128)}, u32[]{:S(2)}) copy-start(f32[8,128]{1,0:T(8,128)} %get-tuple-element.9) | copy-start | bytes 12292
